TPU v7x, 512 devices: a whole 4x4x16 slice. The times are simulated.
512 devices in a mesh: gx: 32 (over x_lo, z), gy: 16 (over y, x_hi, core).
Axes of the slice: x: 4 (x_hi: 2, x_lo: 2; x = x_hi * 2 + x_lo), y: 4, z: 16, core: 2. Of those that a mesh axis runs over, the one named last changes fastest.
Arguments:
- velocity: float32 [3, 1, 4096, 10240], P(None, None, 'gy', 'gx'), may hold values from -12 to 12
- grid_x: float32 [33], replicated, may hold values from 0.05 to 1
- grid_y: float32 [4096, 33], P('gy'), may hold values from 0.05 to 1
- test_x: float32 [33], replicated, may hold values from 0.05 to 1
- test_y: float32 [4096, 33], P('gy'), may hold values from 0.05 to 1
Outputs:
- subgrid: float32 [6, 1, 4096, 10240], P(None, None, 'gy', 'gx')
- germano: float32 [6, 1, 4096, 10240], P(None, None, 'gy', 'gx')
All inputs are finite; a program needn't handle non-finite values.
Results may differ from a plain program's by a relative error of at most 0.0001.
Values sent between devices are 32-bit elements; how exact they have to be, the bound alone decides.
No kernel may reach another device: no remote copies, remote signals or barrier semaphores. Data moves between devices by JAX's collectives and lax.ppermute only.
A program may use at most 64 MiB of HBM per device.

v0:
```python
import jax
import jax.numpy as jnp
from jax import lax
from jax.experimental import pallas as pl
from jax.experimental.pallas import tpu as pltpu
from jax.sharding import PartitionSpec as P

BF = jnp.bfloat16
F32 = jnp.float32
HALF = 16
TAPS = 33
HALO = 32
NX = 320
NY = 256
RING = 384
NX_READ = NX + 2 * HALO
NX_COARSE = NX + 2 * HALF
QUARTER = NX_READ // 4
PAIRS = [(0, 0), (0, 1), (0, 2), (1, 1), (1, 2), (2, 2)]
VMEM = pl.BlockSpec(memory_space=pltpu.VMEM)
SMEM = pl.BlockSpec(memory_space=pltpu.SMEM)
ANY = pl.BlockSpec(memory_space=pl.ANY)


def split(x):
    hi = x.astype(BF)
    return hi, (x - hi.astype(F32)).astype(BF)


def read_kernel(v_ref, left_ref, right_ref, table_ref, read, to_low, to_high):
    for f in range(3):
        read[f, 0:HALO] = left_ref[f]
        read[f, HALO : HALO + NX] = v_ref[f]
        read[f, HALO + NX :] = right_ref[f]
        quarters = [pl.ds(QUARTER * q, QUARTER) for q in range(4)]
        to_low[f, 0:QUARTER] = jnp.concatenate([read[f, r, 0:HALO] for r in quarters], axis=1)
        to_high[f, 0:QUARTER] = jnp.concatenate([read[f, r, NY - HALO : NY] for r in quarters], axis=1)
    for f in range(3):
        to_low[f, QUARTER:] = jnp.zeros((HALF, 128), F32)
        to_high[f, QUARTER:] = jnp.zeros((HALF, 128), F32)
    to_low[0, QUARTER:, 0:TAPS] = table_ref[0:HALF, :]
    to_high[0, QUARTER:, 0:TAPS] = table_ref[NY - HALF : NY, :]


def make_read(velocity, left, right, table):
    edge = jax.ShapeDtypeStruct((3, QUARTER + HALF, 128), F32)
    return pl.pallas_call(
        read_kernel,
        out_shape=[jax.ShapeDtypeStruct((3, NX_READ, NY), F32), edge, edge],
        in_specs=[VMEM] * 4,
        out_specs=[VMEM] * 3,
        compiler_params=pltpu.CompilerParams(vmem_limit_bytes=16 << 20),
    )(velocity, left, right, table)


def norm_y(table, first_row, total_rows):
    row = first_row + lax.broadcasted_iota(jnp.int32, table.shape, 0)
    tap = lax.broadcasted_iota(jnp.int32, table.shape, 1)
    source = row + tap - HALF
    masked = jnp.where((source >= 0) & (source < total_rows) & (tap < TAPS), table, 0.0)
    total = jnp.sum(masked, axis=1, keepdims=True)
    inside = (row[:, :1] >= 0) & (row[:, :1] < total_rows)
    return masked / jnp.where(inside, total, 1.0)


def rolled(part, offset, lanes):
    m = part.shape[0]
    wide = jnp.concatenate([part, jnp.zeros((m, lanes - 128), F32)], axis=1)
    return pltpu.roll(wide, offset % lanes, 1, stride=1, stride_axis=0)


def y_matrix(weights, lane, out, row):
    m = weights.shape[0]
    high = weights.astype(BF).astype(F32)
    hi = rolled(high, lane - HALF, RING)
    lo = rolled(weights - high, lane - HALF, RING)
    edge = hi[:, NY:] + pltpu.roll(hi[:, NY:], 64, 1)
    parts = [hi[:, :NY], hi[:, :NY], lo[:, :NY], edge, lo[:, NY:]]
    out[row : row + m, :] = jnp.concatenate(parts, axis=1).astype(BF)


def lanes_of(hi, lo):
    lane = lax.broadcasted_iota(jnp.int32, (hi.shape[0], 128), 1)
    outer = (lane < HALO) | (lane >= 128 - HALO)
    low = pltpu.roll(lo[:, NY:].astype(F32), 64, 1).astype(BF)
    edge = jnp.where(outer, hi[:, NY:], low)
    return jnp.concatenate([hi[:, :NY], lo[:, :NY], hi[:, :NY], edge, hi[:, NY:]], axis=1)


def filter_y(x, matrix):
    return lax.dot_general(
        lanes_of(*split(x)), matrix, (((1,), (1,)), ((), ())), preferred_element_type=F32
    )


def x_taps(taps_ref, rows):
    lane = lax.broadcasted_iota(jnp.int32, (rows, 128), 1)
    taps = jnp.zeros((rows, 128), F32)
    for t in range(TAPS):
        taps = jnp.where(lane == t, taps_ref[t], taps)
    return taps / jnp.sum(taps, axis=1, keepdims=True)


def x_matrix(taps_ref, m):
    k = m + 2 * HALF
    lanes = -(-3 * k // 128) * 128
    taps = x_taps(taps_ref, m)
    high = taps.astype(BF).astype(F32)
    low = taps - high
    total = rolled(high, 0, lanes) + rolled(high, k, lanes) + rolled(low, 2 * k, lanes)
    return total.astype(BF)


def filter_x(matrix, x, start, m):
    k = m + 2 * HALF
    hi, lo = split(x[start : start + k])
    spare = matrix.shape[1] - 3 * k
    parts = [hi, lo, hi]
    if spare:
        parts.append(jnp.zeros((spare, x.shape[1]), BF))
    return jnp.dot(matrix, jnp.concatenate(parts, axis=0), preferred_element_type=F32)


def main_kernel(
    grid_x, test_x, center, low_ref, high_ref, grid_y, test_y, subgrid, germano,
    read, smooth, coarse, tested, y_grid, y_test, tab_g, tab_t, buf_s, buf_g, sems,
):
    first_row = lax.axis_index("gy") * NY
    total_rows = lax.axis_size("gy") * NY
    tab_g[...] = jnp.zeros_like(tab_g)
    tab_t[...] = jnp.zeros_like(tab_t)
    tab_g[0:HALF, 0:TAPS] = low_ref[0, QUARTER:, 0:TAPS]
    tab_g[HALF : HALF + NY, 0:TAPS] = grid_y[...]
    tab_g[HALF + NY :, 0:TAPS] = high_ref[0, QUARTER:, 0:TAPS]
    tab_t[:, 0:TAPS] = test_y[...]
    w_grid = norm_y(tab_g[...], first_row - HALF, total_rows)
    w_test = norm_y(tab_t[...], first_row, total_rows)
    for s in (0, 128):
        y_matrix(w_grid[HALF + s : HALF + s + 128], s, y_grid, s)
        y_matrix(w_test[s : s + 128], s, y_test, s)
    y_grid[NY:, :] = jnp.zeros((128, 4 * NY), BF)
    y_matrix(w_grid[HALF + NY :], NY, y_grid, NY)
    y_matrix(w_grid[0:HALF], RING - HALF, y_grid, RING - HALF)
    x_grid = {m: x_matrix(grid_x, m) for m in (128, 96, 64)}
    x_test = {m: x_matrix(test_x, m) for m in (128, 64)}
    copies = []

    def send(buffer, out, p, sem):
        copy = pltpu.make_async_copy(buffer.at[p], out.at[p], sem)
        copy.start()
        copies.append(copy)

    for f in range(3):
        read[f, :, 0:NY] = center[f]
        for q in range(4):
            lanes = slice(HALO * q, HALO * (q + 1))
            read[f, QUARTER * q : QUARTER * (q + 1), NY:] = jnp.concatenate(
                [high_ref[f, 0:QUARTER, lanes], jnp.zeros((QUARTER, 64), F32), low_ref[f, 0:QUARTER, lanes]], axis=1
            )
    for f in range(3):
        for start, m in ((0, 128), (128, 128), (256, 96)):
            smooth[f, start : start + m] = filter_x(x_grid[m], read[f], start, m)
        coarse[f] = filter_y(smooth[f], y_grid[...])
    for p, (i, j) in enumerate(PAIRS):
        product = read[i, HALF : HALF + NX_COARSE] * read[j, HALF : HALF + NX_COARSE]
        for start, m in ((0, 128), (128, 128), (256, 64)):
            smooth[3 + p, start : start + m] = filter_x(x_grid[m], product, start, m)
        own = slice(HALF, HALF + NX)
        stress = filter_y(smooth[3 + p, 0:NX], y_grid[0:NY, :])
        buf_s[p] = stress - coarse[i, own, 0:NY] * coarse[j, own, 0:NY]
        send(buf_s, subgrid, p, sems.at[p])
    for f in range(9):
        field = coarse[f] if f < 3 else coarse[PAIRS[f - 3][0]] * coarse[PAIRS[f - 3][1]]
        for start, m in ((0, 128), (128, 128), (256, 64)):
            smooth[f, start : start + m] = filter_x(x_test[m], field, start, m)
        result = filter_y(smooth[f, 0:NX], y_test[...])
        if f < 3:
            tested[f] = result
        else:
            i, j = PAIRS[f - 3]
            buf_g[f - 3] = result - tested[i] * tested[j]
            send(buf_g, germano, f - 3, sems.at[3 + f])
    for copy in copies:
        copy.wait()


def main(grid_x, test_x, center, low, high, grid_y, test_y):
    out = jax.ShapeDtypeStruct((6, NX, NY), F32)
    return pl.pallas_call(
        main_kernel,
        out_shape=[out, out],
        in_specs=[SMEM, SMEM] + [VMEM] * 5,
        out_specs=[ANY, ANY],
        scratch_shapes=[
            pltpu.VMEM((3, NX_READ, RING), F32),
            pltpu.VMEM((9, NX_COARSE, RING), F32),
            pltpu.VMEM((3, NX_COARSE, RING), F32),
            pltpu.VMEM((3, NX, NY), F32),
            pltpu.VMEM((RING, 4 * NY), BF),
            pltpu.VMEM((NY, 4 * NY), BF),
            pltpu.VMEM((NY + 2 * HALF, 128), F32),
            pltpu.VMEM((NY, 128), F32),
            pltpu.VMEM((6, NX, NY), F32),
            pltpu.VMEM((6, NX, NY), F32),
            pltpu.SemaphoreType.DMA((12,)),
        ],
        compiler_params=pltpu.CompilerParams(vmem_limit_bytes=40 << 20),
    )(grid_x, test_x, center, low, high, grid_y, test_y)


def shifts(axis, periodic):
    count = lax.axis_size(axis)
    up = [(i, i + 1) for i in range(count - 1)]
    if periodic:
        up.append((count - 1, 0))
    return up, [(b, a) for a, b in up]


def local(velocity, grid_x, grid_y, test_x, test_y):
    velocity = velocity.reshape(3, NY, NX).swapaxes(1, 2)
    up, down = shifts("gx", True)
    left = lax.ppermute(velocity[:, NX - HALO :], "gx", up)
    right = lax.ppermute(velocity[:, :HALO], "gx", down)
    center, to_low, to_high = make_read(velocity, left, right, grid_y)
    up, down = shifts("gy", False)
    low = lax.ppermute(to_high, "gy", up)
    high = lax.ppermute(to_low, "gy", down)
    outs = main(grid_x, test_x, center, low, high, grid_y, test_y)
    return tuple(out.swapaxes(1, 2).reshape(6, 1, NY, NX) for out in outs)


def solution(mesh):
    placed = (P(None, None, "gy", "gx"), P(), P("gy", None), P(), P("gy", None))
    return jax.shard_map(
        local,
        mesh=mesh,
        in_specs=placed,
        out_specs=(P(None, None, "gy", "gx"), P(None, None, "gy", "gx")),
        check_vma=False,
    )
```

profile of v0, /device:TPU:1, one launch (start us, length us, event | category | flops | bytes accessed | tf_op | source)
XLA Modules:
  0.0 47.6 jit_solution(6828164410616583938)
XLA Ops:
  0.6 0.0 copy-start.2
  0.6 0.0 copy-start.1
  0.6 1.0 %fusion = (f32[3,32,256]{2,1,0:T(8,128)S(1)}, f32[3,32,256]{2,1,0:T(8,128)S(1)}) fusion(f32[3,320,256]{2,1,0:T(8,128)} %bitcast.13), kind=kLoop, calls=%fused_computation | loop fusion | bytes 393216 | tf_op jit(solution)/shard_map/slice | solution.py:223
  1.6 12.9 %collective-permute-start.1 = (f32[3,32,256]{2,1,0:T(8,128)S(1)}, f32[3,32,256]{2,1,0:T(8,128)S(1)}, u32[]{:S(2)}, u32[]{:S(2)}) collective-permute-start(f32[3,32,256]{2,1,0:T(8,128)S(1)} %get-tuple-element.14), channel_id=1, source_target_pairs={{16,0},{32,16},{48,32},{64,48},{80,64},{96,80},{112,96},{128,112},... | collective-permute-start | bytes 294920 | tf_op jit(solution)/shard_map/ppermute | solution.py:223
  14.5 1.9 %collective-permute-start = (f32[3,32,256]{2,1,0:T(8,128)S(1)}, f32[3,32,256]{2,1,0:T(8,128)S(1)}, u32[]{:S(2)}, u32[]{:S(2)}) collective-permute-start(f32[3,32,256]{2,1,0:T(8,128)S(1)} %get-tuple-element.15), channel_id=1, source_target_pairs={{0,16},{16,32},{32,48},{48,64},{64,80},{80,96},{96,112},{112,128},... | collective-permute-start | bytes 294920 | tf_op jit(solution)/shard_map/ppermute | solution.py:222
  16.4 0.9 %copy.7.table_ref.grid_y = f32[256,33]{1,0:T(8,128)S(1)} copy(f32[256,33]{0,1:T(8,128)} %param.7) | data formatting | bytes 67584 | tf_op args[2]
  17.3 0.0 collective-permute-done.1.right_ref
  17.3 4.6 %collective-permute-done.left_ref = f32[3,32,256]{2,1,0:T(8,128)S(1)} collective-permute-done((f32[3,32,256]{2,1,0:T(8,128)S(1)}, f32[3,32,256]{2,1,0:T(8,128)S(1)}, u32[]{:S(2)}, u32[]{:S(2)}) %collective-permute-start) | collective-permute-done | bytes 98336 | tf_op jit(solution)/shard_map/ppermute | solution.py:222
  22.0 0.0 copy-start
  22.0 1.2 %copy-done = f32[3,1,256,320]{2,3,1,0:T(8,128)S(1)} copy-done((f32[3,1,256,320]{2,3,1,0:T(8,128)S(1)}, f32[3,1,256,320]{2,3,1,0:T(8,128)}, u32[]{:S(2)}) %copy-start) | copy-done | bytes 983064
  23.2 0.3 shard_map.68
  23.5 6.3 %collective-permute-start.2 = (f32[3,112,128]{2,1,0:T(8,128)S(1)}, f32[3,112,128]{2,1,0:T(8,128)S(1)}, u32[]{:S(2)}, u32[]{:S(2)}) collective-permute-start(f32[3,112,128]{2,1,0:T(8,128)S(1)} %get-tuple-element.8), channel_id=1, source_target_pairs={{0,1},{1,2},{2,3},{3,4},{4,5},{5,6},{6,7},{7,8},{8,9},{9,10},{10,1... | collective-permute-start | bytes 516104 | tf_op jit(solution)/shard_map/ppermute | solution.py:226
  29.8 1.9 %collective-permute-start.3 = (f32[3,112,128]{2,1,0:T(8,128)S(1)}, f32[3,112,128]{2,1,0:T(8,128)S(1)}, u32[]{:S(2)}, u32[]{:S(2)}) collective-permute-start(f32[3,112,128]{2,1,0:T(8,128)S(1)} %get-tuple-element.9), channel_id=1, source_target_pairs={{1,0},{2,1},{3,2},{4,3},{5,4},{6,5},{7,6},{8,7},{9,8},{10,9},{11,1... | collective-permute-start | bytes 516104 | tf_op jit(solution)/shard_map/ppermute | solution.py:227
  31.8 0.9 %copy.9.test_y = f32[256,33]{1,0:T(8,128)S(1)} copy(f32[256,33]{0,1:T(8,128)} %param.9) | data formatting | bytes 67584 | tf_op args[4]
  32.7 0.0 collective-permute-done.2.low_ref
  32.7 5.4 %collective-permute-done.3.high_ref = f32[3,112,128]{2,1,0:T(8,128)S(1)} collective-permute-done((f32[3,112,128]{2,1,0:T(8,128)S(1)}, f32[3,112,128]{2,1,0:T(8,128)S(1)}, u32[]{:S(2)}, u32[]{:S(2)}) %collective-permute-start.3) | collective-permute-done | bytes 172064 | tf_op jit(solution)/shard_map/ppermute | solution.py:227
  38.1 0.0 copy-done.2
  38.1 0.0 copy-done.1
  38.1 9.5 %shard_map.69 = (f32[6,320,256]{2,1,0:T(8,128)}, f32[6,320,256]{2,1,0:T(8,128)}) custom-call(f32[33]{0:T(128)S(1)} %copy-done.1, f32[33]{0:T(128)S(1)} %copy-done.2, f32[3,384,256]{2,1,0:T(8,128)S(1)} %get-tuple-element.7.center, f32[3,112,128]{2,1,0:T(8,128)S(1)} %collective-permute-done.2.low_ref, f32[3,112,128]{2,1,0:T(8,128)S(1)} %collective-permute-done.3.high_ref, ...), custom_call_target="tpu_custom_call" | custom-call | tf_op jit(solution)/shard_map/pallas_call | solution.py:189
Async XLA Ops:
  0.6 37.4 %copy-start.2 = (f32[33]{0:T(128)S(1)}, f32[33]{0:T(128)}, u32[]{:S(2)}) copy-start(f32[33]{0:T(128)} %test_x.1) | copy-start | bytes 400
  0.6 37.4 %copy-start.1 = (f32[33]{0:T(128)S(1)}, f32[33]{0:T(128)}, u32[]{:S(2)}) copy-start(f32[33]{0:T(128)} %grid_x.1) | copy-start | bytes 400
  1.6 15.7 %collective-permute-start.1 = (f32[3,32,256]{2,1,0:T(8,128)S(1)}, f32[3,32,256]{2,1,0:T(8,128)S(1)}, u32[]{:S(2)}, u32[]{:S(2)}) collective-permute-start(f32[3,32,256]{2,1,0:T(8,128)S(1)} %get-tuple-element.14), channel_id=1, source_target_pairs={{16,0},{32,16},{48,32},{64,48},{80,64},{96,80},{112,96},{128,112},... | collective-permute-start | bytes 294920 | tf_op jit(solution)/shard_map/ppermute | solution.py:223
  14.5 7.5 %collective-permute-start = (f32[3,32,256]{2,1,0:T(8,128)S(1)}, f32[3,32,256]{2,1,0:T(8,128)S(1)}, u32[]{:S(2)}, u32[]{:S(2)}) collective-permute-start(f32[3,32,256]{2,1,0:T(8,128)S(1)} %get-tuple-element.15), channel_id=1, source_target_pairs={{0,16},{16,32},{32,48},{48,64},{64,80},{80,96},{96,112},{112,128},... | collective-permute-start | bytes 294920 | tf_op jit(solution)/shard_map/ppermute | solution.py:222
  22.0 1.2 %copy-start = (f32[3,1,256,320]{2,3,1,0:T(8,128)S(1)}, f32[3,1,256,320]{2,3,1,0:T(8,128)}, u32[]{:S(2)}) copy-start(f32[3,1,256,320]{2,3,1,0:T(8,128)} %param.5) | copy-start | bytes 2949124
  23.5 9.2 %collective-permute-start.2 = (f32[3,112,128]{2,1,0:T(8,128)S(1)}, f32[3,112,128]{2,1,0:T(8,128)S(1)}, u32[]{:S(2)}, u32[]{:S(2)}) collective-permute-start(f32[3,112,128]{2,1,0:T(8,128)S(1)} %get-tuple-element.8), channel_id=1, source_target_pairs={{0,1},{1,2},{2,3},{3,4},{4,5},{5,6},{6,7},{7,8},{8,9},{9,10},{10,1... | collective-permute-start | bytes 516104 | tf_op jit(solution)/shard_map/ppermute | solution.py:226
  29.8 8.2 %collective-permute-start.3 = (f32[3,112,128]{2,1,0:T(8,128)S(1)}, f32[3,112,128]{2,1,0:T(8,128)S(1)}, u32[]{:S(2)}, u32[]{:S(2)}) collective-permute-start(f32[3,112,128]{2,1,0:T(8,128)S(1)} %get-tuple-element.9), channel_id=1, source_target_pairs={{1,0},{2,1},{3,2},{4,3},{5,4},{6,5},{7,6},{8,7},{9,8},{10,9},{11,1... | collective-permute-start | bytes 516104 | tf_op jit(solution)/shard_map/ppermute | solution.py:227
where the time goes:
time: 48 us; the launch traced here: 47.6 us
  starting transfers between devices  23.1 us (48%)
  waiting for transfers between devices  10.1 us (21%)
  Pallas kernels  9.81 us (20%)
  local copies, waits for them, and re-layouts  3.95 us (8%)
  between operations  0.71 us (1%)
    ppermute x1, starting transfers between devices, local(): right = lax.ppermute(velocity[:, :HALO], 'gx', down)  12.9 us
    pallas_call x1, Pallas kernels, main(): pl.pallas_call(main_kernel, out_shape=[out, out], in_specs=[SMEM, SMEM] +...  9.52 us
    ppermute x1, starting transfers between devices, local(): low = lax.ppermute(to_high, 'gy', up)  6.35 us
    ppermute x1, waiting for transfers between devices, local(): high = lax.ppermute(to_low, 'gy', down)  5.4 us
    ppermute x1, waiting for transfers between devices, local(): left = lax.ppermute(velocity[:, NX - HALO:], 'gx', up)  4.64 us
    unnamed x8, local copies, waits for them, and re-layouts  2.98 us
    ppermute x1, starting transfers between devices, local(): left = lax.ppermute(velocity[:, NX - HALO:], 'gx', up)  1.92 us
    ppermute x1, starting transfers between devices, local(): high = lax.ppermute(to_low, 'gy', down)  1.92 us
  transfers between devices with their start and end apart: 4, of which 2 were waited for; matrix products, arithmetic and copies ran while one was open for 4% of the time, Pallas kernels for 0%

commit v1 on v0

v1 whole, which is shorter than its diff:
```python
import jax
import jax.numpy as jnp
from jax import lax
from jax.experimental import pallas as pl
from jax.experimental.pallas import tpu as pltpu
from jax.sharding import PartitionSpec as P

BF = jnp.bfloat16
F32 = jnp.float32
HALF = 16
TAPS = 33
HALO = 32
NX = 320
NY = 256
RING = 384
NX_READ = NX + 2 * HALO
NX_COARSE = NX + 2 * HALF
TAP_ROWS = 40
QUARTER = NX_READ // 4
PAIRS = [(0, 0), (0, 1), (0, 2), (1, 1), (1, 2), (2, 2)]
VMEM = pl.BlockSpec(memory_space=pltpu.VMEM)
SMEM = pl.BlockSpec(memory_space=pltpu.SMEM)
HBM = pl.BlockSpec(memory_space=pltpu.HBM)


def cost(us):
    return pl.CostEstimate(flops=us * 10**9, bytes_accessed=10**6, transcendentals=0)


def split(x):
    hi = x.astype(BF)
    return hi, (x - hi.astype(F32)).astype(BF)


def is_even(axis):
    return lax.rem(lax.axis_index(axis), 2) == 0


def edges(velocity):
    even = is_even("gx")
    low, high = velocity[:, :HALO], velocity[:, NX - HALO :]
    return jnp.where(even, low, high), jnp.where(even, high, low)


def pack_kernel(own, x_first, x_second, taps, first, second, read, table):
    even_x, even_y = is_even("gx"), is_even("gy")
    for f in range(3):
        read[f, HALO : HALO + NX] = own[f]
        read[f, 0:HALO] = jnp.where(even_x, x_first[f], x_second[f])
        read[f, HALO + NX :] = jnp.where(even_x, x_second[f], x_first[f])
        quarters = [pl.ds(QUARTER * q, QUARTER) for q in range(4)]
        low = jnp.concatenate([read[f, r, 0:HALO] for r in quarters], axis=1)
        high = jnp.concatenate([read[f, r, NY - HALO : NY] for r in quarters], axis=1)
        first[QUARTER * f : QUARTER * (f + 1), :] = jnp.where(even_y, low, high)
        second[QUARTER * f : QUARTER * (f + 1), :] = jnp.where(even_y, high, low)
    table[...] = jnp.zeros_like(table)
    table[0:TAPS, :] = taps[...]
    groups = [pl.ds(8 * g, 8) for g in range(TAP_ROWS // 8)]
    spare = jnp.zeros((8, 128 - 2 * TAP_ROWS), F32)
    low = jnp.concatenate([table[r, 0:HALF] for r in groups] + [spare], axis=1)
    high = jnp.concatenate([table[r, NY - HALF : NY] for r in groups] + [spare], axis=1)
    first[3 * QUARTER :, :] = jnp.where(even_y, low, high)
    second[3 * QUARTER :, :] = jnp.where(even_y, high, low)


def pack(own, x_first, x_second, taps):
    edge = jax.ShapeDtypeStruct((3 * QUARTER + 8, 128), F32)
    return pl.pallas_call(
        pack_kernel,
        out_shape=[edge, edge, jax.ShapeDtypeStruct((3, NX_READ, NY), F32)],
        in_specs=[VMEM] * 4,
        out_specs=[VMEM] * 3,
        scratch_shapes=[pltpu.VMEM((TAP_ROWS, NY), F32)],
        compiler_params=pltpu.CompilerParams(vmem_limit_bytes=8 << 20),
        cost_estimate=cost(5),
    )(own, x_first, x_second, taps)


def norm_y(taps, cell, total_cells):
    tap = lax.broadcasted_iota(jnp.int32, taps.shape, 0)
    source = cell + tap - HALF
    masked = jnp.where((source >= 0) & (source < total_cells) & (tap < TAPS), taps, 0.0)
    total = jnp.sum(masked, axis=0, keepdims=True)
    weights = masked / jnp.where(total > 0, total, 1.0)
    high = weights.astype(BF).astype(F32)
    return high, weights - high


def slanted(part, rows, cells):
    x = jnp.concatenate([part, jnp.zeros((rows - part.shape[0], 128), F32)], axis=0)
    lane = lax.broadcasted_iota(jnp.int32, x.shape, 1)
    step = 1
    while step < cells:
        x = jnp.where((lane & step) != 0, pltpu.roll(x, step, 0), x)
        step *= 2
    return x


def rolled(part, offset, lanes):
    m = part.shape[0]
    wide = jnp.concatenate([part, jnp.zeros((m, lanes - 128), F32)], axis=1)
    return pltpu.roll(wide, offset % lanes, 1, stride=1, stride_axis=0)


def y_matrix(taps_ref, first_cell, total_cells, table, out):
    table[...] = jnp.zeros_like(table)
    table[0:TAPS, :] = taps_ref[...]
    out[...] = jnp.zeros_like(out)
    for s in (0, 128):
        cell = first_cell + s + lax.broadcasted_iota(jnp.int32, (TAP_ROWS, 128), 1)
        weights = norm_y(table[:, s : s + 128], cell, total_cells)
        hi, lo = (slanted(part, 128 + 2 * HALF, 128).astype(BF) for part in weights)
        own = slice(HALF, 128 + 2 * HALF) if s == 0 else slice(0, 128 + HALF)
        halo = slice(0, HALF) if s == 0 else slice(128 + HALF, 128 + 2 * HALF)
        row = 0 if s == 0 else 128 - HALF
        halo_row = 128 - HALF if s == 0 else 0
        lanes = slice(s, s + 128)
        for base, part in ((0, hi), (NY, hi), (2 * NY, lo)):
            out[base + row : base + row + 128 + HALF, lanes] = part[own]
        for base, part in ((halo_row, hi), ((halo_row + 64) % 128, hi), (128 + halo_row, lo)):
            out[3 * NY + base : 3 * NY + base + HALF, lanes] = part[halo]


def outer_matrix(higher, lower, first_cell, total_cells, out):
    lane = lax.broadcasted_iota(jnp.int32, (TAP_ROWS, 128), 1)
    groups = [slice(HALF * g, HALF * (g + 1)) for g in range(TAP_ROWS // 8)]
    spare = jnp.zeros((8, 128 - 2 * HALF), F32)
    taps = [jnp.concatenate([higher[:, g], spare, lower[:, g]], axis=1) for g in groups]
    cell = first_cell + jnp.where(lane < 64, NY + lane, lane - 128)
    weights = norm_y(jnp.concatenate(taps, axis=0), cell, total_cells)
    hi, lo = (slanted(part, 3 * HALF, HALF) for part in weights)
    low_side = lax.broadcasted_iota(jnp.int32, hi.shape, 1) >= 64
    out[...] = jnp.zeros_like(out)
    ends = []
    for part in (hi, lo):
        high_end = jnp.where(low_side, 0.0, part).astype(BF)
        low_end = jnp.where(low_side, part, 0.0).astype(BF)
        ends.append((high_end[HALF:], low_end[0:HALO], high_end[0:HALF], low_end[HALO:]))
    for base, part in ((0, 0), (64, 0), (128, 1)):
        out[base : base + HALO, :] = ends[part][0]
    for base, part in ((96, 0), (32, 0), (128 + 96, 1)):
        out[base : base + HALO, :] = ends[part][1]
    for base, part in ((112, 0), (16, 0), (48, 1)):
        out[256 + base : 256 + base + HALF, :] = ends[part][2]
    for base, part in ((0, 0), (32, 0), (64, 1)):
        out[256 + base : 256 + base + HALF, :] = ends[part][3]


def halo_lanes(hi, lo):
    lane = lax.broadcasted_iota(jnp.int32, hi.shape, 1)
    outer = (lane < HALO) | (lane >= 128 - HALO)
    return jnp.where(outer, hi, pltpu.roll(lo.astype(F32), 64, 1).astype(BF))


def lanes_of(hi, lo):
    own = [hi[:, :NY], lo[:, :NY], hi[:, :NY]]
    return jnp.concatenate(own + [halo_lanes(hi[:, NY:], lo[:, NY:]), hi[:, NY:]], axis=1)


def times(left, matrix):
    return jnp.dot(left, matrix, preferred_element_type=F32)


def x_taps(taps_ref, rows):
    lane = lax.broadcasted_iota(jnp.int32, (rows, 128), 1)
    taps = jnp.zeros((rows, 128), F32)
    for t in range(TAPS):
        taps = jnp.where(lane == t, taps_ref[t], taps)
    return taps / jnp.sum(taps, axis=1, keepdims=True)


def x_matrix(taps_ref, m):
    k = m + 2 * HALF
    lanes = -(-3 * k // 128) * 128
    taps = x_taps(taps_ref, m)
    high = taps.astype(BF).astype(F32)
    low = taps - high
    total = rolled(high, 0, lanes) + rolled(high, k, lanes) + rolled(low, 2 * k, lanes)
    return total.astype(BF)


def filter_x(matrix, x, start, m):
    k = m + 2 * HALF
    hi, lo = split(x[start : start + k])
    spare = matrix.shape[1] - 3 * k
    parts = [hi, lo, hi]
    if spare:
        parts.append(jnp.zeros((spare, x.shape[1]), BF))
    return jnp.dot(matrix[...], jnp.concatenate(parts, axis=0), preferred_element_type=F32)


def matrix_kernel(grid_x, test_x, grid_y, test_y, y_grid, y_test, *rest):
    first_cell = lax.axis_index("gy") * NY
    total_cells = lax.axis_size("gy") * NY
    table = rest[-1]
    for out, (taps, m) in zip(rest[:-1], X_PARTS):
        out[...] = x_matrix((grid_x, test_x)[taps], m)
    y_matrix(grid_y, first_cell, total_cells, table, y_grid)
    y_matrix(test_y, first_cell, total_cells, table, y_test)


X_PARTS = [(0, 128), (0, 96), (0, 64), (1, 128), (1, 64)]


def matrices(grid_x, test_x, grid_y, test_y):
    return pl.pallas_call(
        matrix_kernel,
        out_shape=[
            jax.ShapeDtypeStruct((4 * NY, NY), BF),
            jax.ShapeDtypeStruct((4 * NY, NY), BF),
        ]
        + [jax.ShapeDtypeStruct((m, -(-3 * (m + 2 * HALF) // 128) * 128), BF) for _, m in X_PARTS],
        in_specs=[SMEM, SMEM, VMEM, VMEM],
        out_specs=[VMEM] * (2 + len(X_PARTS)),
        scratch_shapes=[pltpu.VMEM((TAP_ROWS, NY), F32)],
        compiler_params=pltpu.CompilerParams(vmem_limit_bytes=8 << 20),
        cost_estimate=cost(2),
    )(grid_x, test_x, grid_y, test_y)


VELOCITY_TILES = ((0, 128), (128, 128), (256, 96))
INNER_TILES = ((0, 128), (128, 128), (256, 64))


STARTS = [NX_COARSE * f for f in range(3)] + [3 * NX_COARSE + NX * p for p in range(6)]
STACK = 3 * NX_COARSE + 6 * NX


def own_kernel(read, x128, x96, x64, y_grid, part, near, hi, lo):
    x_grid = {128: x128, 96: x96, 64: x64}
    for f in range(9):
        if f < 3:
            field, tiles = read[f], VELOCITY_TILES
        else:
            i, j = PAIRS[f - 3]
            inner = slice(HALF, HALF + NX_COARSE)
            field, tiles = read[i, inner] * read[j, inner], INNER_TILES
        for start, m in tiles:
            rows = slice(STARTS[f] + start, STARTS[f] + start + m)
            hi[rows], lo[rows] = split(filter_x(x_grid[m], field, start, m))
        rows = slice(STARTS[f], STARTS[f] + (NX_COARSE if f < 3 else NX))
        if f < 3:
            near[f] = near_lanes(hi[rows], lo[rows])
    part[...] = times(jnp.concatenate([hi[...], lo[...], hi[...]], axis=1), y_grid[0 : 3 * NY])


def near_lanes(hi, lo):
    lane = lax.broadcasted_iota(jnp.int32, (hi.shape[0], 128), 1)
    ends = [jnp.where(lane < HALF, x[:, 0:128], x[:, 128:NY]).astype(F32) for x in (hi, lo)]
    low, again = pltpu.roll(ends[1], 32, 1), pltpu.roll(ends[0], 64, 1)
    ends = jnp.where((lane < HALF) | (lane >= 128 - HALF), ends[0], jnp.where(lane < 48, low, again))
    return ends.astype(BF)


def filter_own(read, x_grid, y_grid):
    return pl.pallas_call(
        own_kernel,
        out_shape=[
            jax.ShapeDtypeStruct((STACK, NY), F32),
            jax.ShapeDtypeStruct((3, NX_COARSE, 128), BF),
        ],
        in_specs=[VMEM] * 5,
        out_specs=[VMEM] * 2,
        scratch_shapes=[pltpu.VMEM((STACK, NY), BF), pltpu.VMEM((STACK, NY), BF)],
        compiler_params=pltpu.CompilerParams(vmem_limit_bytes=12 << 20),
        cost_estimate=cost(3),
    )(read, *x_grid, y_grid)


def main_kernel(
    part, near, y_first, y_second, y_grid, y_test, x128, x96, x64, t128, t64, subgrid, germano,
    edge, smooth, coarse, tested, y_outer, buf_s, buf_g, sems,
):
    even = is_even("gy")
    x_grid = {128: x128, 96: x96, 64: x64}
    x_test = {128: t128, 64: t64}

    def from_neighbours(rows):
        one, two = y_first[rows, :], y_second[rows, :]
        return jnp.where(even, two, one), jnp.where(even, one, two)

    higher, lower = from_neighbours(slice(3 * QUARTER, 3 * QUARTER + 8))
    cells = lax.axis_index("gy") * NY, lax.axis_size("gy") * NY
    outer_matrix(higher, lower, *cells, y_outer)
    copies = []

    def send(buffer, out, p, sem):
        copy = pltpu.make_async_copy(buffer.at[p], out.at[p], sem)
        copy.start()
        copies.append(copy)

    for f in range(3):
        higher, lower = from_neighbours(slice(QUARTER * f, QUARTER * (f + 1)))
        for q in range(4):
            lanes = slice(HALO * q, HALO * (q + 1))
            edge[QUARTER * q : QUARTER * (q + 1), 128 * f : 128 * (f + 1)] = jnp.concatenate(
                [higher[:, lanes], jnp.zeros((QUARTER, 64), F32), lower[:, lanes]], axis=1
            )
    for start, m in VELOCITY_TILES:
        smooth[start : start + m, 0:384] = filter_x(x_grid[m], edge, start, m)
    fields = [edge[HALF : HALF + NX_COARSE, 128 * f : 128 * (f + 1)] for f in range(3)]
    products = jnp.concatenate([fields[i] * fields[j] for i, j in PAIRS], axis=1)
    for start, m in INNER_TILES:
        smooth[start : start + m, 384:] = filter_x(x_grid[m], products, start, m)

    def halo_factor(f, rows):
        hi, lo = split(smooth[0:rows, 128 * f : 128 * (f + 1)])
        return jnp.concatenate([halo_lanes(hi, lo), hi], axis=1)

    for f in range(3):
        left = halo_factor(f, NX_COARSE)
        coarse[f, :, 0:NY] = part[STARTS[f] : STARTS[f] + NX_COARSE] + times(left, y_grid[3 * NY :])
        coarse[f, :, NY:] = times(jnp.concatenate([left, near[f]], axis=1), y_outer[...])
    own = slice(HALF, HALF + NX)
    for p, (i, j) in enumerate(PAIRS):
        rows = slice(STARTS[3 + p], STARTS[3 + p] + NX)
        stress = part[rows] + times(halo_factor(3 + p, NX), y_grid[3 * NY :])
        buf_s[p] = stress - coarse[i, own, 0:NY] * coarse[j, own, 0:NY]
        send(buf_s, subgrid, p, sems.at[p])
    for f in range(9):
        field = coarse[f] if f < 3 else coarse[PAIRS[f - 3][0]] * coarse[PAIRS[f - 3][1]]
        parts = [split(filter_x(x_test[m], field, start, m)) for start, m in INNER_TILES]
        hi = jnp.concatenate([part[0] for part in parts], axis=0)
        lo = jnp.concatenate([part[1] for part in parts], axis=0)
        result = times(lanes_of(hi, lo), y_test[...])
        if f < 3:
            tested[f] = result
        else:
            i, j = PAIRS[f - 3]
            buf_g[f - 3] = result - tested[i] * tested[j]
            send(buf_g, germano, f - 3, sems.at[3 + f])
    for copy in copies:
        copy.wait()


def main(part, near, y_first, y_second, y_grid, y_test, x_parts):
    out = jax.ShapeDtypeStruct((6, NX, NY), F32)
    return pl.pallas_call(
        main_kernel,
        out_shape=[out, out],
        in_specs=[VMEM] * (6 + len(x_parts)),
        out_specs=[HBM, HBM],
        scratch_shapes=[
            pltpu.VMEM((NX_READ, 3 * 128), F32),
            pltpu.VMEM((NX_COARSE, 9 * 128), F32),
            pltpu.VMEM((3, NX_COARSE, RING), F32),
            pltpu.VMEM((3, NX, NY), F32),
            pltpu.VMEM((3 * 128, 128), BF),
            pltpu.VMEM((6, NX, NY), F32),
            pltpu.VMEM((6, NX, NY), F32),
            pltpu.SemaphoreType.DMA((12,)),
        ],
        compiler_params=pltpu.CompilerParams(vmem_limit_bytes=24 << 20),
    )(part, near, y_first, y_second, y_grid, y_test, *x_parts)


def swaps(axis, first, periodic):
    count = lax.axis_size(axis)
    last = count if periodic else count - 1
    pairs = [(i, (i + 1) % count) for i in range(first, last, 2)]
    return pairs + [(b, a) for a, b in pairs]


def local(velocity, grid_x, grid_y, test_x, test_y):
    velocity = velocity.reshape(3, NY, NX).swapaxes(1, 2)
    first, second = edges(velocity)
    x_first = lax.ppermute(first, "gx", swaps("gx", 1, True))
    x_second = lax.ppermute(second, "gx", swaps("gx", 0, True))
    y_grid, y_test, *x_parts = matrices(grid_x, test_x, grid_y.T, test_y.T)
    first, second, read = pack(velocity, x_first, x_second, grid_y.T)
    y_first = lax.ppermute(first, "gy", swaps("gy", 1, False))
    y_second = lax.ppermute(second, "gy", swaps("gy", 0, False))
    part, near = filter_own(read, x_parts[:3], y_grid)
    outs = main(part, near, y_first, y_second, y_grid, y_test, x_parts)
    return tuple(out.swapaxes(1, 2).reshape(6, 1, NY, NX) for out in outs)


def solution(mesh):
    placed = (P(None, None, "gy", "gx"), P(), P("gy", None), P(), P("gy", None))
    return jax.shard_map(
        local,
        mesh=mesh,
        in_specs=placed,
        out_specs=(P(None, None, "gy", "gx"), P(None, None, "gy", "gx")),
        check_vma=False,
    )
```

time: 48 us -> 38.4 us (0.80)
  waiting for transfers between devices: 10.1 us -> 0.01 us
  local copies, waits for them, and re-layouts: 3.95 us -> 2.86 us
  other arithmetic: 0 us -> 0.96 us
  Pallas kernels: 9.81 us -> 10.5 us
    ppermute x4, waiting for transfers between devices: 10.1 us -> 0.01 us  [the longest x1 0.01 us: local(): x_second = lax.ppermute(second, 'gx', swaps('gx', 0, True))]
    slice x1 -> x0, local copies, waits for them, and re-layouts: 0.97 us -> none  [local(): right = lax.ppermute(velocity[:, :HALO], 'gx', down)]
    select_n x0 -> x1, other arithmetic: none -> 0.96 us  [edges(): return (jnp.where(even, low, high), jnp.where(even, high, low))]
    pallas_call x2 -> x4, Pallas kernels: 9.81 us -> 10.5 us  [the longest x1 6.33 us: main(): pl.pallas_call(main_kernel, out_shape=[out, out], in_specs=[VMEM] * (6 +...]
    unnamed x8 -> x10, local copies, waits for them, and re-layouts: 2.98 us -> 2.86 us
  transfers between devices with their start and end apart: 4 -> 4, of which waited for: 2 -> 0; matrix products, arithmetic and copies ran while one was open for 4% -> 0% of each run, Pallas kernels for 0% -> 10%
where the time goes in v1:
time: 38.4 us; the launch traced here: 38 us
  starting transfers between devices  22.9 us (60%)
  Pallas kernels  10.5 us (27%)
  local copies, waits for them, and re-layouts  2.86 us (7%)
  other arithmetic  0.96 us (2%)
  between operations  0.75 us (2%)
    ppermute x1, starting transfers between devices, local(): x_first = lax.ppermute(first, 'gx', swaps('gx', 1, True))  11.1 us
    pallas_call x1, Pallas kernels, main(): pl.pallas_call(main_kernel, out_shape=[out, out], in_specs=[VMEM] * (6 +...  6.33 us
    ppermute x1, starting transfers between devices, local(): y_first = lax.ppermute(first, 'gy', swaps('gy', 1, False))  5.48 us
    ppermute x1, starting transfers between devices, local(): x_second = lax.ppermute(second, 'gx', swaps('gx', 0, True))  4.38 us
    unnamed x10, local copies, waits for them, and re-layouts  2.86 us
    pallas_call x1, Pallas kernels, filter_own(): pl.pallas_call(own_kernel, out_shape=[jax.ShapeDtypeStruct((STACK, NY), F...  2.64 us
    ppermute x1, starting transfers between devices, local(): y_second = lax.ppermute(second, 'gy', swaps('gy', 0, False))  1.92 us
    pallas_call x1, Pallas kernels, matrices(): pl.pallas_call(matrix_kernel, out_shape=[jax.ShapeDtypeStruct((4 * NY, NY...  1.21 us
  transfers between devices with their start and end apart: 4, of which 0 were waited for; matrix products, arithmetic and copies ran while one was open for 0% of the time, Pallas kernels for 10%

profile of v1, /device:TPU:1, one launch (start us, length us, event | category | flops | bytes accessed | tf_op | source)
XLA Modules:
  0.0 38.0 jit_solution(6526226445162437325)
XLA Ops:
  0.6 1.0 %slice_select_fusion = (f32[3,32,256]{2,1,0:T(8,128)S(1)}, f32[3,32,256]{2,1,0:T(8,128)S(1)}) fusion(f32[3,320,256]{2,1,0:T(8,128)} %bitcast.15, pred[]{:T(512)S(6)} %eq.3), kind=kLoop, calls=%fused_computation | loop fusion | flops 49152 | bytes 393217 | tf_op jit(solution)/shard_map/jit(_where)/select_n | solution.py:42
  1.6 4.4 %collective-permute-start.1 = (f32[3,32,256]{2,1,0:T(8,128)S(1)}, f32[3,32,256]{2,1,0:T(8,128)S(1)}, u32[]{:S(2)}, u32[]{:S(2)}) collective-permute-start(f32[3,32,256]{2,1,0:T(8,128)S(1)} %get-tuple-element.32), channel_id=1, source_target_pairs={{0,16},{32,48},{64,80},{96,112},{128,144},{160,176},{192,208},{224... | collective-permute-start | bytes 294920 | tf_op jit(solution)/shard_map/ppermute | solution.py:368
  6.0 11.1 %collective-permute-start = (f32[3,32,256]{2,1,0:T(8,128)S(1)}, f32[3,32,256]{2,1,0:T(8,128)S(1)}, u32[]{:S(2)}, u32[]{:S(2)}) collective-permute-start(f32[3,32,256]{2,1,0:T(8,128)S(1)} %get-tuple-element.33), channel_id=1, source_target_pairs={{16,32},{48,64},{80,96},{112,128},{144,160},{176,192},{208,224},{2... | collective-permute-start | bytes 294920 | tf_op jit(solution)/shard_map/ppermute | solution.py:367
  17.1 0.0 copy-start.1
  17.1 0.8 %copy-done.1 = f32[256,33]{0,1:T(8,128)S(1)} copy-done((f32[256,33]{0,1:T(8,128)S(1)}, f32[256,33]{0,1:T(8,128)}, u32[]{:S(2)}) %copy-start.1) | copy-done | bytes 33816
  17.9 0.0 copy-start.2
  17.9 0.8 %copy-done.2 = f32[256,33]{0,1:T(8,128)S(1)} copy-done((f32[256,33]{0,1:T(8,128)S(1)}, f32[256,33]{0,1:T(8,128)}, u32[]{:S(2)}) %copy-start.2) | copy-done | bytes 33816
  18.7 0.0 copy-start.3
  18.7 0.7 %copy-done.3 = f32[33]{0:T(128)S(1)} copy-done((f32[33]{0:T(128)S(1)}, f32[33]{0:T(128)}, u32[]{:S(2)}) %copy-start.3) | copy-done | bytes 156
  19.4 0.0 copy-start.4
  19.4 0.7 %copy-done.4 = f32[33]{0:T(128)S(1)} copy-done((f32[33]{0:T(128)S(1)}, f32[33]{0:T(128)}, u32[]{:S(2)}) %copy-start.4) | copy-done | bytes 156
  20.0 0.0 copy-start
  20.0 1.2 %shard_map.69 = (bf16[1024,256]{1,0:T(8,128)(2,1)S(1)}, bf16[1024,256]{1,0:T(8,128)(2,1)S(1)}, bf16[128,512]{1,0:T(8,128)(2,1)S(1)}, bf16[96,384]{1,0:T(8,128)(2...) custom-call(f32[33]{0:T(128)S(1)} %copy-done.3, f32[33]{0:T(128)S(1)} %copy-done.4, ...), custom_call_target="tpu_custom_call" | custom-call | flops 2000000000 | bytes 1000000 | tf_op jit(solution)/shard_map/pallas_call | solution.py:206
  21.2 0.0 collective-permute-done.1.x_second
  21.2 0.0 collective-permute-done.x_first
  21.2 0.0 copy-done
  21.3 0.3 shard_map.68
  21.6 5.5 %collective-permute-start.2 = (f32[296,128]{1,0:T(8,128)S(1)}, f32[296,128]{1,0:T(8,128)S(1)}, u32[]{:S(2)}, u32[]{:S(2)}) collective-permute-start(f32[296,128]{1,0:T(8,128)S(1)} %get-tuple-element.23), channel_id=1, source_target_pairs={{1,2},{3,4},{5,6},{7,8},{9,10},{11,12},{13,14},{2,1},{4,3},{6,5},{... | collective-permute-start | bytes 454664 | tf_op jit(solution)/shard_map/ppermute | solution.py:371
  27.1 1.9 %collective-permute-start.3 = (f32[296,128]{1,0:T(8,128)S(1)}, f32[296,128]{1,0:T(8,128)S(1)}, u32[]{:S(2)}, u32[]{:S(2)}) collective-permute-start(f32[296,128]{1,0:T(8,128)S(1)} %get-tuple-element.24), channel_id=1, source_target_pairs={{0,1},{2,3},{4,5},{6,7},{8,9},{10,11},{12,13},{14,15},{1,0},{3,2},... | collective-permute-start | bytes 454664 | tf_op jit(solution)/shard_map/ppermute | solution.py:372
  29.0 2.6 %shard_map.70 = (f32[2976,256]{1,0:T(8,128)S(1)}, bf16[3,352,128]{2,1,0:T(8,128)(2,1)S(1)}) custom-call(f32[3,384,256]{2,1,0:T(8,128)S(1)} %get-tuple-element.16.read, bf16[128,512]{1,0:T(8,128)(2,1)S(1)} %get-tuple-element.17.x128, bf16[96,384]{1,0:T(8,128)(2,1)S(1)} %get-tuple-element.18.x96, bf16[64,384]{1,0:T(8,128)(2,1)S(1)} %get-tuple-element.19.x64, ...), custom_call_target="tpu_custom_call" | custom-call | flops 3000000000 | bytes 1000000 | tf_op jit(solution)/shard_map/pallas_call | solution.py:256
  31.6 0.0 collective-permute-done.2.y_first
  31.7 0.0 collective-permute-done.3.y_second
  31.7 6.3 %shard_map.71 = (f32[6,320,256]{2,1,0:T(8,128)}, f32[6,320,256]{2,1,0:T(8,128)}) custom-call(f32[2976,256]{1,0:T(8,128)S(1)} %get-tuple-element.21.part, bf16[3,352,128]{2,1,0:T(8,128)(2,1)S(1)} %get-tuple-element.22.near, f32[296,128]{1,0:T(8,128)S(1)} %collective-permute-done.2.y_first, f32[296,128]{1,0:T(8,128)S(1)} %collective-permute-done.3.y_second, ...), custom_call_target="tpu_custom_call" | custom-call | tf_op jit(solution)/shard_map/pallas_call | solution.py:338
Async XLA Ops:
  1.6 19.6 %collective-permute-start.1 = (f32[3,32,256]{2,1,0:T(8,128)S(1)}, f32[3,32,256]{2,1,0:T(8,128)S(1)}, u32[]{:S(2)}, u32[]{:S(2)}) collective-permute-start(f32[3,32,256]{2,1,0:T(8,128)S(1)} %get-tuple-element.32), channel_id=1, source_target_pairs={{0,16},{32,48},{64,80},{96,112},{128,144},{160,176},{192,208},{224... | collective-permute-start | bytes 294920 | tf_op jit(solution)/shard_map/ppermute | solution.py:368
  6.0 15.2 %collective-permute-start = (f32[3,32,256]{2,1,0:T(8,128)S(1)}, f32[3,32,256]{2,1,0:T(8,128)S(1)}, u32[]{:S(2)}, u32[]{:S(2)}) collective-permute-start(f32[3,32,256]{2,1,0:T(8,128)S(1)} %get-tuple-element.33), channel_id=1, source_target_pairs={{16,32},{48,64},{80,96},{112,128},{144,160},{176,192},{208,224},{2... | collective-permute-start | bytes 294920 | tf_op jit(solution)/shard_map/ppermute | solution.py:367
  17.1 0.8 %copy-start.1 = (f32[256,33]{0,1:T(8,128)S(1)}, f32[256,33]{0,1:T(8,128)}, u32[]{:S(2)}) copy-start(f32[256,33]{0,1:T(8,128)} %param.9) | copy-start | bytes 101380
  17.9 0.8 %copy-start.2 = (f32[256,33]{0,1:T(8,128)S(1)}, f32[256,33]{0,1:T(8,128)}, u32[]{:S(2)}) copy-start(f32[256,33]{0,1:T(8,128)} %param.7) | copy-start | bytes 101380
  18.7 0.7 %copy-start.3 = (f32[33]{0:T(128)S(1)}, f32[33]{0:T(128)}, u32[]{:S(2)}) copy-start(f32[33]{0:T(128)} %grid_x.1) | copy-start | bytes 400
  19.4 0.7 %copy-start.4 = (f32[33]{0:T(128)S(1)}, f32[33]{0:T(128)}, u32[]{:S(2)}) copy-start(f32[33]{0:T(128)} %test_x.1) | copy-start | bytes 400
  20.0 1.2 %copy-start = (f32[3,1,256,320]{2,3,1,0:T(8,128)S(1)}, f32[3,1,256,320]{2,3,1,0:T(8,128)}, u32[]{:S(2)}) copy-start(f32[3,1,256,320]{2,3,1,0:T(8,128)} %param.5) | copy-start | bytes 2949124
  21.6 10.1 %collective-permute-start.2 = (f32[296,128]{1,0:T(8,128)S(1)}, f32[296,128]{1,0:T(8,128)S(1)}, u32[]{:S(2)}, u32[]{:S(2)}) collective-permute-start(f32[296,128]{1,0:T(8,128)S(1)} %get-tuple-element.23), channel_id=1, source_target_pairs={{1,2},{3,4},{5,6},{7,8},{9,10},{11,12},{13,14},{2,1},{4,3},{6,5},{... | collective-permute-start | bytes 454664 | tf_op jit(solution)/shard_map/ppermute | solution.py:371
  27.1 4.6 %collective-permute-start.3 = (f32[296,128]{1,0:T(8,128)S(1)}, f32[296,128]{1,0:T(8,128)S(1)}, u32[]{:S(2)}, u32[]{:S(2)}) collective-permute-start(f32[296,128]{1,0:T(8,128)S(1)} %get-tuple-element.24), channel_id=1, source_target_pairs={{0,1},{2,3},{4,5},{6,7},{8,9},{10,11},{12,13},{14,15},{1,0},{3,2},... | collective-permute-start | bytes 454664 | tf_op jit(solution)/shard_map/ppermute | solution.py:372

commit v2 on v1

--- a/solution.py
+++ b/solution.py
@@ -213,7 +213,7 @@
         in_specs=[SMEM, SMEM, VMEM, VMEM],
         out_specs=[VMEM] * (2 + len(X_PARTS)),
         scratch_shapes=[pltpu.VMEM((TAP_ROWS, NY), F32)],
-        compiler_params=pltpu.CompilerParams(vmem_limit_bytes=8 << 20),
+        compiler_params=pltpu.CompilerParams(vmem_limit_bytes=61 << 20),
         cost_estimate=cost(2),
     )(grid_x, test_x, grid_y, test_y)
 
@@ -269,7 +269,7 @@
 
 def main_kernel(
     part, near, y_first, y_second, y_grid, y_test, x128, x96, x64, t128, t64, subgrid, germano,
-    edge, smooth, coarse, tested, y_outer, buf_s, buf_g, sems,
+    edge, smooth, coarse, tested, y_outer, buf_s, buf_g, own_hi, own_lo, halo, sems,
 ):
     even = is_even("gy")
     x_grid = {128: x128, 96: x96, 64: x64}
@@ -319,16 +319,23 @@
         send(buf_s, subgrid, p, sems.at[p])
     for f in range(9):
         field = coarse[f] if f < 3 else coarse[PAIRS[f - 3][0]] * coarse[PAIRS[f - 3][1]]
-        parts = [split(filter_x(x_test[m], field, start, m)) for start, m in INNER_TILES]
-        hi = jnp.concatenate([part[0] for part in parts], axis=0)
-        lo = jnp.concatenate([part[1] for part in parts], axis=0)
-        result = times(lanes_of(hi, lo), y_test[...])
-        if f < 3:
-            tested[f] = result
-        else:
-            i, j = PAIRS[f - 3]
-            buf_g[f - 3] = result - tested[i] * tested[j]
-            send(buf_g, germano, f - 3, sems.at[3 + f])
+        for start, m in INNER_TILES:
+            rows = slice(NX * f + start, NX * f + start + m)
+            hi, lo = split(filter_x(x_test[m], field, start, m))
+            own_hi[rows], own_lo[rows] = hi[:, :NY], lo[:, :NY]
+            halo[rows] = jnp.concatenate([halo_lanes(hi[:, NY:], lo[:, NY:]), hi[:, NY:]], axis=1)
+    for first, last in ((0, 3), (3, 6), (6, 9)):
+        rows = slice(NX * first, NX * last)
+        left = jnp.concatenate([own_hi[rows], own_lo[rows], own_hi[rows], halo[rows]], axis=1)
+        results = times(left, y_test[...])
+        for f in range(first, last):
+            result = results[NX * (f - first) : NX * (f - first + 1)]
+            if f < 3:
+                tested[f] = result
+            else:
+                i, j = PAIRS[f - 3]
+                buf_g[f - 3] = result - tested[i] * tested[j]
+                send(buf_g, germano, f - 3, sems.at[3 + f])
     for copy in copies:
         copy.wait()
 
@@ -348,6 +355,9 @@
             pltpu.VMEM((3 * 128, 128), BF),
             pltpu.VMEM((6, NX, NY), F32),
             pltpu.VMEM((6, NX, NY), F32),
+            pltpu.VMEM((9 * NX, NY), BF),
+            pltpu.VMEM((9 * NX, NY), BF),
+            pltpu.VMEM((9 * NX, NY), BF),
             pltpu.SemaphoreType.DMA((12,)),
         ],
         compiler_params=pltpu.CompilerParams(vmem_limit_bytes=24 << 20),

time: 38.4 us -> 36.7 us (0.956)
  local copies, waits for them, and re-layouts: 2.86 us -> 0.04 us
  Pallas kernels: 10.5 us -> 11.7 us
    unnamed x10 -> x18, local copies, waits for them, and re-layouts: 2.86 us -> 0.04 us
    pallas_call x1, Pallas kernels: 1.21 us -> 2.53 us  [matrices(): pl.pallas_call(matrix_kernel, out_shape=[jax.ShapeDtypeStruct((4 * NY, NY...]
  transfers between devices with their start and end apart: 4 -> 4, of which waited for: 0 -> 0; matrix products, arithmetic and copies ran while one was open for 0% -> 0% of each run, Pallas kernels for 10% -> 14%
where the time goes in v2:
time: 36.7 us; the launch traced here: 36.4 us
  starting transfers between devices  22.9 us (62%)
  Pallas kernels  11.7 us (32%)
  other arithmetic  0.96 us (3%)
  between operations  0.84 us (2%)
    ppermute x1, starting transfers between devices, local(): x_first = lax.ppermute(first, 'gx', swaps('gx', 1, True))  11.1 us
    pallas_call x1, Pallas kernels, main(): pl.pallas_call(main_kernel, out_shape=[out, out], in_specs=[VMEM] * (6 +...  6.18 us
    ppermute x1, starting transfers between devices, local(): y_first = lax.ppermute(first, 'gy', swaps('gy', 1, False))  5.48 us
    ppermute x1, starting transfers between devices, local(): x_second = lax.ppermute(second, 'gx', swaps('gx', 0, True))  4.38 us
    pallas_call x1, Pallas kernels, filter_own(): pl.pallas_call(own_kernel, out_shape=[jax.ShapeDtypeStruct((STACK, NY), F...  2.64 us
    pallas_call x1, Pallas kernels, matrices(): pl.pallas_call(matrix_kernel, out_shape=[jax.ShapeDtypeStruct((4 * NY, NY...  2.53 us
    ppermute x1, starting transfers between devices, local(): y_second = lax.ppermute(second, 'gy', swaps('gy', 0, False))  1.92 us
    select_n x1, other arithmetic, edges(): return (jnp.where(even, low, high), jnp.where(even, high, low))  0.96 us
  transfers between devices with their start and end apart: 4, of which 0 were waited for; matrix products, arithmetic and copies ran while one was open for 0% of the time, Pallas kernels for 14%

profile of v2, /device:TPU:1, one launch (start us, length us, event | category | flops | bytes accessed | tf_op | source)
XLA Modules:
  0.0 36.4 jit_solution(13479102206011754415)
XLA Ops:
  0.6 1.0 %slice_select_fusion = (f32[3,32,256]{2,1,0:T(8,128)S(1)}, f32[3,32,256]{2,1,0:T(8,128)S(1)}) fusion(f32[3,320,256]{2,1,0:T(8,128)} %bitcast.15, pred[]{:T(512)S(6)} %eq.3), kind=kLoop, calls=%fused_computation | loop fusion | flops 49152 | bytes 393217 | tf_op jit(solution)/shard_map/jit(_where)/select_n | solution.py:42
  1.6 4.4 %collective-permute-start.1 = (f32[3,32,256]{2,1,0:T(8,128)S(1)}, f32[3,32,256]{2,1,0:T(8,128)S(1)}, u32[]{:S(2)}, u32[]{:S(2)}) collective-permute-start(f32[3,32,256]{2,1,0:T(8,128)S(1)} %get-tuple-element.32), channel_id=1, source_target_pairs={{0,16},{32,48},{64,80},{96,112},{128,144},{160,176},{192,208},{224... | collective-permute-start | bytes 294920 | tf_op jit(solution)/shard_map/ppermute | solution.py:378
  6.0 11.1 %collective-permute-start = (f32[3,32,256]{2,1,0:T(8,128)S(1)}, f32[3,32,256]{2,1,0:T(8,128)S(1)}, u32[]{:S(2)}, u32[]{:S(2)}) collective-permute-start(f32[3,32,256]{2,1,0:T(8,128)S(1)} %get-tuple-element.33), channel_id=1, source_target_pairs={{16,32},{48,64},{80,96},{112,128},{144,160},{176,192},{208,224},{2... | collective-permute-start | bytes 294920 | tf_op jit(solution)/shard_map/ppermute | solution.py:377
  17.1 0.0 copy-start.7
  17.1 0.0 copy-start.8
  17.2 2.5 %shard_map.69 = (bf16[1024,256]{1,0:T(8,128)(2,1)}, bf16[1024,256]{1,0:T(8,128)(2,1)}, bf16[128,512]{1,0:T(8,128)(2,1)}, bf16[96,384]{1,0:T(8,128)(2,1)}, bf16[6...) custom-call(f32[33]{0:T(128)} %grid_x.1, f32[33]{0:T(128)} %test_x.1, f32[33,256]{1,0:T(8,128)} %bitcast.17, ...), custom_call_target="tpu_custom_call" | custom-call | flops 2000000000 | bytes 1000000 | tf_op jit(solution)/shard_map/pallas_call | solution.py:206
  19.7 0.0 copy-start
  19.7 0.0 copy-start.2
  19.7 0.0 copy-start.4
  19.7 0.0 copy-start.5
  19.7 0.0 collective-permute-done.1.x_second
  19.7 0.0 collective-permute-done.x_first
  19.7 0.0 copy-done.7
  19.7 0.0 copy-done.8
  19.7 0.3 shard_map.68
  20.1 5.5 %collective-permute-start.2 = (f32[296,128]{1,0:T(8,128)S(1)}, f32[296,128]{1,0:T(8,128)S(1)}, u32[]{:S(2)}, u32[]{:S(2)}) collective-permute-start(f32[296,128]{1,0:T(8,128)S(1)} %get-tuple-element.23), channel_id=1, source_target_pairs={{1,2},{3,4},{5,6},{7,8},{9,10},{11,12},{13,14},{2,1},{4,3},{6,5},{... | collective-permute-start | bytes 454664 | tf_op jit(solution)/shard_map/ppermute | solution.py:381
  25.6 1.9 %collective-permute-start.3 = (f32[296,128]{1,0:T(8,128)S(1)}, f32[296,128]{1,0:T(8,128)S(1)}, u32[]{:S(2)}, u32[]{:S(2)}) collective-permute-start(f32[296,128]{1,0:T(8,128)S(1)} %get-tuple-element.24), channel_id=1, source_target_pairs={{0,1},{2,3},{4,5},{6,7},{8,9},{10,11},{12,13},{14,15},{1,0},{3,2},... | collective-permute-start | bytes 454664 | tf_op jit(solution)/shard_map/ppermute | solution.py:382
  27.5 0.0 copy-done
  27.5 0.0 copy-done.2
  27.5 0.0 copy-done.4
  27.5 0.0 copy-done.5
  27.5 0.0 copy-start.1
  27.5 0.0 copy-start.3
  27.5 0.0 copy-start.6
  27.6 2.6 %shard_map.70 = (f32[2976,256]{1,0:T(8,128)S(1)}, bf16[3,352,128]{2,1,0:T(8,128)(2,1)S(1)}) custom-call(f32[3,384,256]{2,1,0:T(8,128)S(1)} %get-tuple-element.16.read, bf16[128,512]{1,0:T(8,128)(2,1)S(1)} %copy-done.2, bf16[96,384]{1,0:T(8,128)(2,1)S(1)} %copy-done.4, bf16[64,384]{1,0:T(8,128)(2,1)S(1)} %copy-done.5, bf16[1024,256]{1,0:T(8,128)(2,1)S(1)} %copy-done), custom_call_target="tpu_custom_call" | custom-call | flops 3000000000 | bytes 1000000 | tf_op jit(solution)/shard_map/pallas_call | solution.py:256
  30.2 0.0 collective-permute-done.2.y_first
  30.2 0.0 collective-permute-done.3.y_second
  30.2 0.0 copy-done.1
  30.2 0.0 copy-done.3
  30.2 0.0 copy-done.6
  30.3 6.2 %shard_map.71 = (f32[6,320,256]{2,1,0:T(8,128)}, f32[6,320,256]{2,1,0:T(8,128)}) custom-call(f32[2976,256]{1,0:T(8,128)S(1)} %get-tuple-element.21.part, bf16[3,352,128]{2,1,0:T(8,128)(2,1)S(1)} %get-tuple-element.22.near, f32[296,128]{1,0:T(8,128)S(1)} %collective-permute-done.2.y_first, f32[296,128]{1,0:T(8,128)S(1)} %collective-permute-done.3.y_second, ...), custom_call_target="tpu_custom_call" | custom-call | tf_op jit(solution)/shard_map/pallas_call | solution.py:345
Async XLA Ops:
  1.6 18.1 %collective-permute-start.1 = (f32[3,32,256]{2,1,0:T(8,128)S(1)}, f32[3,32,256]{2,1,0:T(8,128)S(1)}, u32[]{:S(2)}, u32[]{:S(2)}) collective-permute-start(f32[3,32,256]{2,1,0:T(8,128)S(1)} %get-tuple-element.32), channel_id=1, source_target_pairs={{0,16},{32,48},{64,80},{96,112},{128,144},{160,176},{192,208},{224... | collective-permute-start | bytes 294920 | tf_op jit(solution)/shard_map/ppermute | solution.py:378
  6.0 13.7 %collective-permute-start = (f32[3,32,256]{2,1,0:T(8,128)S(1)}, f32[3,32,256]{2,1,0:T(8,128)S(1)}, u32[]{:S(2)}, u32[]{:S(2)}) collective-permute-start(f32[3,32,256]{2,1,0:T(8,128)S(1)} %get-tuple-element.33), channel_id=1, source_target_pairs={{16,32},{48,64},{80,96},{112,128},{144,160},{176,192},{208,224},{2... | collective-permute-start | bytes 294920 | tf_op jit(solution)/shard_map/ppermute | solution.py:377
  17.1 2.6 %copy-start.7 = (f32[3,1,256,320]{2,3,1,0:T(8,128)S(1)}, f32[3,1,256,320]{2,3,1,0:T(8,128)}, u32[]{:S(2)}) copy-start(f32[3,1,256,320]{2,3,1,0:T(8,128)} %param.5) | copy-start | bytes 2949124
  17.1 2.6 %copy-start.8 = (f32[256,33]{0,1:T(8,128)S(1)}, f32[256,33]{0,1:T(8,128)}, u32[]{:S(2)}) copy-start(f32[256,33]{0,1:T(8,128)} %param.7) | copy-start | bytes 101380
  19.7 7.8 %copy-start = (bf16[1024,256]{1,0:T(8,128)(2,1)S(1)}, bf16[1024,256]{1,0:T(8,128)(2,1)}, u32[]{:S(2)}) copy-start(bf16[1024,256]{1,0:T(8,128)(2,1)} %get-tuple-element.20.y_grid) | copy-start | bytes 1572868
  19.7 7.8 %copy-start.2 = (bf16[128,512]{1,0:T(8,128)(2,1)S(1)}, bf16[128,512]{1,0:T(8,128)(2,1)}, u32[]{:S(2)}) copy-start(bf16[128,512]{1,0:T(8,128)(2,1)} %get-tuple-element.17.x128) | copy-start | bytes 393220
  19.7 7.8 %copy-start.4 = (bf16[96,384]{1,0:T(8,128)(2,1)S(1)}, bf16[96,384]{1,0:T(8,128)(2,1)}, u32[]{:S(2)}) copy-start(bf16[96,384]{1,0:T(8,128)(2,1)} %get-tuple-element.18.x96) | copy-start | bytes 221188
  19.7 7.8 %copy-start.5 = (bf16[64,384]{1,0:T(8,128)(2,1)S(1)}, bf16[64,384]{1,0:T(8,128)(2,1)}, u32[]{:S(2)}) copy-start(bf16[64,384]{1,0:T(8,128)(2,1)} %get-tuple-element.19.x64) | copy-start | bytes 147460
  20.1 10.1 %collective-permute-start.2 = (f32[296,128]{1,0:T(8,128)S(1)}, f32[296,128]{1,0:T(8,128)S(1)}, u32[]{:S(2)}, u32[]{:S(2)}) collective-permute-start(f32[296,128]{1,0:T(8,128)S(1)} %get-tuple-element.23), channel_id=1, source_target_pairs={{1,2},{3,4},{5,6},{7,8},{9,10},{11,12},{13,14},{2,1},{4,3},{6,5},{... | collective-permute-start | bytes 454664 | tf_op jit(solution)/shard_map/ppermute | solution.py:381
  25.6 4.7 %collective-permute-start.3 = (f32[296,128]{1,0:T(8,128)S(1)}, f32[296,128]{1,0:T(8,128)S(1)}, u32[]{:S(2)}, u32[]{:S(2)}) collective-permute-start(f32[296,128]{1,0:T(8,128)S(1)} %get-tuple-element.24), channel_id=1, source_target_pairs={{0,1},{2,3},{4,5},{6,7},{8,9},{10,11},{12,13},{14,15},{1,0},{3,2},... | collective-permute-start | bytes 454664 | tf_op jit(solution)/shard_map/ppermute | solution.py:382
  27.5 2.7 %copy-start.1 = (bf16[1024,256]{1,0:T(8,128)(2,1)S(1)}, bf16[1024,256]{1,0:T(8,128)(2,1)}, u32[]{:S(2)}) copy-start(bf16[1024,256]{1,0:T(8,128)(2,1)} %get-tuple-element.25.y_test) | copy-start | bytes 1572868
  27.5 2.7 %copy-start.3 = (bf16[128,512]{1,0:T(8,128)(2,1)S(1)}, bf16[128,512]{1,0:T(8,128)(2,1)}, u32[]{:S(2)}) copy-start(bf16[128,512]{1,0:T(8,128)(2,1)} %get-tuple-element.26.t128) | copy-start | bytes 393220
  27.5 2.7 %copy-start.6 = (bf16[64,384]{1,0:T(8,128)(2,1)S(1)}, bf16[64,384]{1,0:T(8,128)(2,1)}, u32[]{:S(2)}) copy-start(bf16[64,384]{1,0:T(8,128)(2,1)} %get-tuple-element.27.t64) | copy-start | bytes 147460

commit v3 on v2

--- a/solution.py
+++ b/solution.py
@@ -152,9 +152,23 @@
     return jnp.where(outer, hi, pltpu.roll(lo.astype(F32), 64, 1).astype(BF))
 
 
-def lanes_of(hi, lo):
-    own = [hi[:, :NY], lo[:, :NY], hi[:, :NY]]
-    return jnp.concatenate(own + [halo_lanes(hi[:, NY:], lo[:, NY:]), hi[:, NY:]], axis=1)
+def packed(tiles):
+    total = tiles[0]
+    for q, tile in enumerate(tiles[1:], 1):
+        total = total + pltpu.roll(tile, HALO * q, 1)
+    return total
+
+
+def unpacked(tile, count):
+    hi, lo = (part.astype(F32) for part in split(tile))
+    lane = lax.broadcasted_iota(jnp.int32, tile.shape, 1)
+    outer = (lane < HALO) | (lane >= 128 - HALO)
+    factors = []
+    for q in range(count):
+        high = pltpu.roll(hi, 128 - HALO * q, 1) if q else hi
+        low = pltpu.roll(lo, (64 - HALO * q) % 128, 1) if q != 2 else lo
+        factors.append(jnp.concatenate([jnp.where(outer, high, low), high], axis=1).astype(BF))
+    return factors
 
 
 def times(left, matrix):
@@ -268,7 +282,7 @@
 
 
 def main_kernel(
-    part, near, y_first, y_second, y_grid, y_test, x128, x96, x64, t128, t64, subgrid, germano,
+    part, ends, y_first, y_second, y_grid, y_test, x128, x96, x64, t128, t64, subgrid, germano,
     edge, smooth, coarse, tested, y_outer, buf_s, buf_g, own_hi, own_lo, halo, sems,
 ):
     even = is_even("gy")
@@ -298,8 +312,12 @@
             )
     for start, m in VELOCITY_TILES:
         smooth[start : start + m, 0:384] = filter_x(x_grid[m], edge, start, m)
+    lane = lax.broadcasted_iota(jnp.int32, (NX_COARSE, 128), 1)
+    near = (lane < HALF) | (lane >= 128 - HALF)
     fields = [edge[HALF : HALF + NX_COARSE, 128 * f : 128 * (f + 1)] for f in range(3)]
-    products = jnp.concatenate([fields[i] * fields[j] for i, j in PAIRS], axis=1)
+    fields = [jnp.where(near, field, 0.0) for field in fields]
+    products = [fields[i] * fields[j] for i, j in PAIRS]
+    products = jnp.concatenate([packed(products[0:4]), packed(products[4:6])], axis=1)
     for start, m in INNER_TILES:
         smooth[start : start + m, 384:] = filter_x(x_grid[m], products, start, m)
 
@@ -310,20 +328,33 @@
     for f in range(3):
         left = halo_factor(f, NX_COARSE)
         coarse[f, :, 0:NY] = part[STARTS[f] : STARTS[f] + NX_COARSE] + times(left, y_grid[3 * NY :])
-        coarse[f, :, NY:] = times(jnp.concatenate([left, near[f]], axis=1), y_outer[...])
+        coarse[f, :, NY:] = times(jnp.concatenate([left, ends[f]], axis=1), y_outer[...])
     own = slice(HALF, HALF + NX)
+    factors = unpacked(smooth[0:NX, 384:512], 4) + unpacked(smooth[0:NX, 512:640], 2)
     for p, (i, j) in enumerate(PAIRS):
         rows = slice(STARTS[3 + p], STARTS[3 + p] + NX)
-        stress = part[rows] + times(halo_factor(3 + p, NX), y_grid[3 * NY :])
+        stress = part[rows] + times(factors[p], y_grid[3 * NY :])
         buf_s[p] = stress - coarse[i, own, 0:NY] * coarse[j, own, 0:NY]
         send(buf_s, subgrid, p, sems.at[p])
+    def test_field(f, lanes):
+        if f < 3:
+            return coarse[f, :, lanes]
+        i, j = PAIRS[f - 3]
+        return coarse[i, :, lanes] * coarse[j, :, lanes]
+
+    groups = [range(0, 4), range(4, 8), range(8, 9)]
+    halos = [packed([test_field(f, slice(NY, RING)) for f in group]) for group in groups]
+    halos = jnp.concatenate(halos, axis=1)
+    for start, m in INNER_TILES:
+        smooth[start : start + m, 0:384] = filter_x(x_test[m], halos, start, m)
+    for n, group in enumerate(groups):
+        for f, factor in zip(group, unpacked(smooth[0:NX, 128 * n : 128 * (n + 1)], len(group))):
+            halo[NX * f : NX * (f + 1)] = factor
     for f in range(9):
-        field = coarse[f] if f < 3 else coarse[PAIRS[f - 3][0]] * coarse[PAIRS[f - 3][1]]
+        field = test_field(f, slice(0, NY))
         for start, m in INNER_TILES:
             rows = slice(NX * f + start, NX * f + start + m)
-            hi, lo = split(filter_x(x_test[m], field, start, m))
-            own_hi[rows], own_lo[rows] = hi[:, :NY], lo[:, :NY]
-            halo[rows] = jnp.concatenate([halo_lanes(hi[:, NY:], lo[:, NY:]), hi[:, NY:]], axis=1)
+            own_hi[rows], own_lo[rows] = split(filter_x(x_test[m], field, start, m))
     for first, last in ((0, 3), (3, 6), (6, 9)):
         rows = slice(NX * first, NX * last)
         left = jnp.concatenate([own_hi[rows], own_lo[rows], own_hi[rows], halo[rows]], axis=1)
@@ -349,7 +380,7 @@
         out_specs=[HBM, HBM],
         scratch_shapes=[
             pltpu.VMEM((NX_READ, 3 * 128), F32),
-            pltpu.VMEM((NX_COARSE, 9 * 128), F32),
+            pltpu.VMEM((NX_COARSE, 5 * 128), F32),
             pltpu.VMEM((3, NX_COARSE, RING), F32),
             pltpu.VMEM((3, NX, NY), F32),
             pltpu.VMEM((3 * 128, 128), BF),

time: 36.7 us -> 36.1 us (0.984)
  Pallas kernels: 11.7 us -> 11.1 us
    pallas_call x1, Pallas kernels: 6.18 us -> 5.64 us  [main(): pl.pallas_call(main_kernel, out_shape=[out, out], in_specs=[VMEM] * (6 +...]
where the time goes in v3:
time: 36.1 us; the launch traced here: 35.9 us
  starting transfers between devices  22.9 us (63%)
  Pallas kernels  11.1 us (31%)
  other arithmetic  0.96 us (3%)
  between operations  0.84 us (2%)
    ppermute x1, starting transfers between devices, local(): x_first = lax.ppermute(first, 'gx', swaps('gx', 1, True))  11.1 us
    pallas_call x1, Pallas kernels, main(): pl.pallas_call(main_kernel, out_shape=[out, out], in_specs=[VMEM] * (6 +...  5.64 us
    ppermute x1, starting transfers between devices, local(): y_first = lax.ppermute(first, 'gy', swaps('gy', 1, False))  5.48 us
    ppermute x1, starting transfers between devices, local(): x_second = lax.ppermute(second, 'gx', swaps('gx', 0, True))  4.38 us
    pallas_call x1, Pallas kernels, filter_own(): pl.pallas_call(own_kernel, out_shape=[jax.ShapeDtypeStruct((STACK, NY), F...  2.64 us
    pallas_call x1, Pallas kernels, matrices(): pl.pallas_call(matrix_kernel, out_shape=[jax.ShapeDtypeStruct((4 * NY, NY...  2.53 us
    ppermute x1, starting transfers between devices, local(): y_second = lax.ppermute(second, 'gy', swaps('gy', 0, False))  1.92 us
    select_n x1, other arithmetic, edges(): return (jnp.where(even, low, high), jnp.where(even, high, low))  0.96 us
  transfers between devices with their start and end apart: 4, of which 0 were waited for; matrix products, arithmetic and copies ran while one was open for 0% of the time, Pallas kernels for 14%

profile of v3, /device:TPU:1, one launch (start us, length us, event | category | flops | bytes accessed | tf_op | source)
XLA Modules:
  0.0 35.9 jit_solution(2302021638700647583)
XLA Ops:
  0.6 1.0 %slice_select_fusion = (f32[3,32,256]{2,1,0:T(8,128)S(1)}, f32[3,32,256]{2,1,0:T(8,128)S(1)}) fusion(f32[3,320,256]{2,1,0:T(8,128)} %bitcast.15, pred[]{:T(512)S(6)} %eq.3), kind=kLoop, calls=%fused_computation | loop fusion | flops 49152 | bytes 393217 | tf_op jit(solution)/shard_map/jit(_where)/select_n | solution.py:42
  1.6 4.4 %collective-permute-start.1 = (f32[3,32,256]{2,1,0:T(8,128)S(1)}, f32[3,32,256]{2,1,0:T(8,128)S(1)}, u32[]{:S(2)}, u32[]{:S(2)}) collective-permute-start(f32[3,32,256]{2,1,0:T(8,128)S(1)} %get-tuple-element.32), channel_id=1, source_target_pairs={{0,16},{32,48},{64,80},{96,112},{128,144},{160,176},{192,208},{224... | collective-permute-start | bytes 294920 | tf_op jit(solution)/shard_map/ppermute | solution.py:409
  6.0 11.1 %collective-permute-start = (f32[3,32,256]{2,1,0:T(8,128)S(1)}, f32[3,32,256]{2,1,0:T(8,128)S(1)}, u32[]{:S(2)}, u32[]{:S(2)}) collective-permute-start(f32[3,32,256]{2,1,0:T(8,128)S(1)} %get-tuple-element.33), channel_id=1, source_target_pairs={{16,32},{48,64},{80,96},{112,128},{144,160},{176,192},{208,224},{2... | collective-permute-start | bytes 294920 | tf_op jit(solution)/shard_map/ppermute | solution.py:408
  17.1 0.0 copy-start.7
  17.1 0.0 copy-start.8
  17.2 2.5 %shard_map.69 = (bf16[1024,256]{1,0:T(8,128)(2,1)}, bf16[1024,256]{1,0:T(8,128)(2,1)}, bf16[128,512]{1,0:T(8,128)(2,1)}, bf16[96,384]{1,0:T(8,128)(2,1)}, bf16[6...) custom-call(f32[33]{0:T(128)} %grid_x.1, f32[33]{0:T(128)} %test_x.1, f32[33,256]{1,0:T(8,128)} %bitcast.17, ...), custom_call_target="tpu_custom_call" | custom-call | flops 2000000000 | bytes 1000000 | tf_op jit(solution)/shard_map/pallas_call | solution.py:220
  19.7 0.0 copy-start
  19.7 0.0 copy-start.2
  19.7 0.0 copy-start.4
  19.7 0.0 copy-start.5
  19.7 0.0 collective-permute-done.1.x_second
  19.7 0.0 collective-permute-done.x_first
  19.7 0.0 copy-done.7
  19.7 0.0 copy-done.8
  19.7 0.3 shard_map.68
  20.1 5.5 %collective-permute-start.2 = (f32[296,128]{1,0:T(8,128)S(1)}, f32[296,128]{1,0:T(8,128)S(1)}, u32[]{:S(2)}, u32[]{:S(2)}) collective-permute-start(f32[296,128]{1,0:T(8,128)S(1)} %get-tuple-element.23), channel_id=1, source_target_pairs={{1,2},{3,4},{5,6},{7,8},{9,10},{11,12},{13,14},{2,1},{4,3},{6,5},{... | collective-permute-start | bytes 454664 | tf_op jit(solution)/shard_map/ppermute | solution.py:412
  25.6 1.9 %collective-permute-start.3 = (f32[296,128]{1,0:T(8,128)S(1)}, f32[296,128]{1,0:T(8,128)S(1)}, u32[]{:S(2)}, u32[]{:S(2)}) collective-permute-start(f32[296,128]{1,0:T(8,128)S(1)} %get-tuple-element.24), channel_id=1, source_target_pairs={{0,1},{2,3},{4,5},{6,7},{8,9},{10,11},{12,13},{14,15},{1,0},{3,2},... | collective-permute-start | bytes 454664 | tf_op jit(solution)/shard_map/ppermute | solution.py:413
  27.5 0.0 copy-done
  27.5 0.0 copy-done.2
  27.5 0.0 copy-done.4
  27.5 0.0 copy-done.5
  27.5 0.0 copy-start.1
  27.5 0.0 copy-start.3
  27.5 0.0 copy-start.6
  27.6 2.6 %shard_map.70 = (f32[2976,256]{1,0:T(8,128)S(1)}, bf16[3,352,128]{2,1,0:T(8,128)(2,1)S(1)}) custom-call(f32[3,384,256]{2,1,0:T(8,128)S(1)} %get-tuple-element.16.read, bf16[128,512]{1,0:T(8,128)(2,1)S(1)} %copy-done.2, bf16[96,384]{1,0:T(8,128)(2,1)S(1)} %copy-done.4, bf16[64,384]{1,0:T(8,128)(2,1)S(1)} %copy-done.5, bf16[1024,256]{1,0:T(8,128)(2,1)S(1)} %copy-done), custom_call_target="tpu_custom_call" | custom-call | flops 3000000000 | bytes 1000000 | tf_op jit(solution)/shard_map/pallas_call | solution.py:270
  30.2 0.0 collective-permute-done.2.y_first
  30.2 0.0 collective-permute-done.3.y_second
  30.2 0.0 copy-done.1
  30.2 0.0 copy-done.3
  30.2 0.0 copy-done.6
  30.3 5.6 %shard_map.71 = (f32[6,320,256]{2,1,0:T(8,128)}, f32[6,320,256]{2,1,0:T(8,128)}) custom-call(f32[2976,256]{1,0:T(8,128)S(1)} %get-tuple-element.21.part, bf16[3,352,128]{2,1,0:T(8,128)(2,1)S(1)} %get-tuple-element.22.ends, f32[296,128]{1,0:T(8,128)S(1)} %collective-permute-done.2.y_first, f32[296,128]{1,0:T(8,128)S(1)} %collective-permute-done.3.y_second, ...), custom_call_target="tpu_custom_call" | custom-call | tf_op jit(solution)/shard_map/pallas_call | solution.py:376
Async XLA Ops:
  1.6 18.1 %collective-permute-start.1 = (f32[3,32,256]{2,1,0:T(8,128)S(1)}, f32[3,32,256]{2,1,0:T(8,128)S(1)}, u32[]{:S(2)}, u32[]{:S(2)}) collective-permute-start(f32[3,32,256]{2,1,0:T(8,128)S(1)} %get-tuple-element.32), channel_id=1, source_target_pairs={{0,16},{32,48},{64,80},{96,112},{128,144},{160,176},{192,208},{224... | collective-permute-start | bytes 294920 | tf_op jit(solution)/shard_map/ppermute | solution.py:409
  6.0 13.7 %collective-permute-start = (f32[3,32,256]{2,1,0:T(8,128)S(1)}, f32[3,32,256]{2,1,0:T(8,128)S(1)}, u32[]{:S(2)}, u32[]{:S(2)}) collective-permute-start(f32[3,32,256]{2,1,0:T(8,128)S(1)} %get-tuple-element.33), channel_id=1, source_target_pairs={{16,32},{48,64},{80,96},{112,128},{144,160},{176,192},{208,224},{2... | collective-permute-start | bytes 294920 | tf_op jit(solution)/shard_map/ppermute | solution.py:408
  17.1 2.6 %copy-start.7 = (f32[3,1,256,320]{2,3,1,0:T(8,128)S(1)}, f32[3,1,256,320]{2,3,1,0:T(8,128)}, u32[]{:S(2)}) copy-start(f32[3,1,256,320]{2,3,1,0:T(8,128)} %param.5) | copy-start | bytes 2949124
  17.1 2.6 %copy-start.8 = (f32[256,33]{0,1:T(8,128)S(1)}, f32[256,33]{0,1:T(8,128)}, u32[]{:S(2)}) copy-start(f32[256,33]{0,1:T(8,128)} %param.7) | copy-start | bytes 101380
  19.7 7.8 %copy-start = (bf16[1024,256]{1,0:T(8,128)(2,1)S(1)}, bf16[1024,256]{1,0:T(8,128)(2,1)}, u32[]{:S(2)}) copy-start(bf16[1024,256]{1,0:T(8,128)(2,1)} %get-tuple-element.20.y_grid) | copy-start | bytes 1572868
  19.7 7.8 %copy-start.2 = (bf16[128,512]{1,0:T(8,128)(2,1)S(1)}, bf16[128,512]{1,0:T(8,128)(2,1)}, u32[]{:S(2)}) copy-start(bf16[128,512]{1,0:T(8,128)(2,1)} %get-tuple-element.17.x128) | copy-start | bytes 393220
  19.7 7.8 %copy-start.4 = (bf16[96,384]{1,0:T(8,128)(2,1)S(1)}, bf16[96,384]{1,0:T(8,128)(2,1)}, u32[]{:S(2)}) copy-start(bf16[96,384]{1,0:T(8,128)(2,1)} %get-tuple-element.18.x96) | copy-start | bytes 221188
  19.7 7.8 %copy-start.5 = (bf16[64,384]{1,0:T(8,128)(2,1)S(1)}, bf16[64,384]{1,0:T(8,128)(2,1)}, u32[]{:S(2)}) copy-start(bf16[64,384]{1,0:T(8,128)(2,1)} %get-tuple-element.19.x64) | copy-start | bytes 147460
  20.1 10.1 %collective-permute-start.2 = (f32[296,128]{1,0:T(8,128)S(1)}, f32[296,128]{1,0:T(8,128)S(1)}, u32[]{:S(2)}, u32[]{:S(2)}) collective-permute-start(f32[296,128]{1,0:T(8,128)S(1)} %get-tuple-element.23), channel_id=1, source_target_pairs={{1,2},{3,4},{5,6},{7,8},{9,10},{11,12},{13,14},{2,1},{4,3},{6,5},{... | collective-permute-start | bytes 454664 | tf_op jit(solution)/shard_map/ppermute | solution.py:412
  25.6 4.7 %collective-permute-start.3 = (f32[296,128]{1,0:T(8,128)S(1)}, f32[296,128]{1,0:T(8,128)S(1)}, u32[]{:S(2)}, u32[]{:S(2)}) collective-permute-start(f32[296,128]{1,0:T(8,128)S(1)} %get-tuple-element.24), channel_id=1, source_target_pairs={{0,1},{2,3},{4,5},{6,7},{8,9},{10,11},{12,13},{14,15},{1,0},{3,2},... | collective-permute-start | bytes 454664 | tf_op jit(solution)/shard_map/ppermute | solution.py:413
  27.5 2.7 %copy-start.1 = (bf16[1024,256]{1,0:T(8,128)(2,1)S(1)}, bf16[1024,256]{1,0:T(8,128)(2,1)}, u32[]{:S(2)}) copy-start(bf16[1024,256]{1,0:T(8,128)(2,1)} %get-tuple-element.25.y_test) | copy-start | bytes 1572868
  27.5 2.7 %copy-start.3 = (bf16[128,512]{1,0:T(8,128)(2,1)S(1)}, bf16[128,512]{1,0:T(8,128)(2,1)}, u32[]{:S(2)}) copy-start(bf16[128,512]{1,0:T(8,128)(2,1)} %get-tuple-element.26.t128) | copy-start | bytes 393220
  27.5 2.7 %copy-start.6 = (bf16[64,384]{1,0:T(8,128)(2,1)S(1)}, bf16[64,384]{1,0:T(8,128)(2,1)}, u32[]{:S(2)}) copy-start(bf16[64,384]{1,0:T(8,128)(2,1)} %get-tuple-element.27.t64) | copy-start | bytes 147460

commit v4 on v3

--- a/solution.py
+++ b/solution.py
@@ -350,12 +350,12 @@
     for n, group in enumerate(groups):
         for f, factor in zip(group, unpacked(smooth[0:NX, 128 * n : 128 * (n + 1)], len(group))):
             halo[NX * f : NX * (f + 1)] = factor
-    for f in range(9):
-        field = test_field(f, slice(0, NY))
-        for start, m in INNER_TILES:
-            rows = slice(NX * f + start, NX * f + start + m)
-            own_hi[rows], own_lo[rows] = split(filter_x(x_test[m], field, start, m))
-    for first, last in ((0, 3), (3, 6), (6, 9)):
+    for first, last in ((0, 3), (3, 6), (6, 8), (8, 9)):
+        for f in range(first, last):
+            field = test_field(f, slice(0, NY))
+            for start, m in INNER_TILES:
+                rows = slice(NX * f + start, NX * f + start + m)
+                own_hi[rows], own_lo[rows] = split(filter_x(x_test[m], field, start, m))
         rows = slice(NX * first, NX * last)
         left = jnp.concatenate([own_hi[rows], own_lo[rows], own_hi[rows], halo[rows]], axis=1)
         results = times(left, y_test[...])

time: 36.1 us -> 36.1 us (level)
  no operation moved by 1% of the time
where the time goes in v4:
time: 36.1 us; the launch traced here: 35.9 us
  starting transfers between devices  22.9 us (63%)
  Pallas kernels  11.1 us (31%)
  other arithmetic  0.96 us (3%)
  between operations  0.84 us (2%)
    ppermute x1, starting transfers between devices, local(): x_first = lax.ppermute(first, 'gx', swaps('gx', 1, True))  11.1 us
    pallas_call x1, Pallas kernels, main(): pl.pallas_call(main_kernel, out_shape=[out, out], in_specs=[VMEM] * (6 +...  5.6 us
    ppermute x1, starting transfers between devices, local(): y_first = lax.ppermute(first, 'gy', swaps('gy', 1, False))  5.48 us
    ppermute x1, starting transfers between devices, local(): x_second = lax.ppermute(second, 'gx', swaps('gx', 0, True))  4.38 us
    pallas_call x1, Pallas kernels, filter_own(): pl.pallas_call(own_kernel, out_shape=[jax.ShapeDtypeStruct((STACK, NY), F...  2.64 us
    pallas_call x1, Pallas kernels, matrices(): pl.pallas_call(matrix_kernel, out_shape=[jax.ShapeDtypeStruct((4 * NY, NY...  2.53 us
    ppermute x1, starting transfers between devices, local(): y_second = lax.ppermute(second, 'gy', swaps('gy', 0, False))  1.92 us
    select_n x1, other arithmetic, edges(): return (jnp.where(even, low, high), jnp.where(even, high, low))  0.96 us
  transfers between devices with their start and end apart: 4, of which 0 were waited for; matrix products, arithmetic and copies ran while one was open for 0% of the time, Pallas kernels for 14%

profile of v4, /device:TPU:1, one launch (start us, length us, event | category | flops | bytes accessed | tf_op | source)
XLA Modules:
  0.0 35.9 jit_solution(18148189027257613929)
XLA Ops:
  0.6 1.0 %slice_select_fusion = (f32[3,32,256]{2,1,0:T(8,128)S(1)}, f32[3,32,256]{2,1,0:T(8,128)S(1)}) fusion(f32[3,320,256]{2,1,0:T(8,128)} %bitcast.15, pred[]{:T(512)S(6)} %eq.3), kind=kLoop, calls=%fused_computation | loop fusion | flops 49152 | bytes 393217 | tf_op jit(solution)/shard_map/jit(_where)/select_n | solution.py:42
  1.6 4.4 %collective-permute-start.1 = (f32[3,32,256]{2,1,0:T(8,128)S(1)}, f32[3,32,256]{2,1,0:T(8,128)S(1)}, u32[]{:S(2)}, u32[]{:S(2)}) collective-permute-start(f32[3,32,256]{2,1,0:T(8,128)S(1)} %get-tuple-element.32), channel_id=1, source_target_pairs={{0,16},{32,48},{64,80},{96,112},{128,144},{160,176},{192,208},{224... | collective-permute-start | bytes 294920 | tf_op jit(solution)/shard_map/ppermute | solution.py:409
  6.0 11.1 %collective-permute-start = (f32[3,32,256]{2,1,0:T(8,128)S(1)}, f32[3,32,256]{2,1,0:T(8,128)S(1)}, u32[]{:S(2)}, u32[]{:S(2)}) collective-permute-start(f32[3,32,256]{2,1,0:T(8,128)S(1)} %get-tuple-element.33), channel_id=1, source_target_pairs={{16,32},{48,64},{80,96},{112,128},{144,160},{176,192},{208,224},{2... | collective-permute-start | bytes 294920 | tf_op jit(solution)/shard_map/ppermute | solution.py:408
  17.1 0.0 copy-start.7
  17.1 0.0 copy-start.8
  17.2 2.5 %shard_map.69 = (bf16[1024,256]{1,0:T(8,128)(2,1)}, bf16[1024,256]{1,0:T(8,128)(2,1)}, bf16[128,512]{1,0:T(8,128)(2,1)}, bf16[96,384]{1,0:T(8,128)(2,1)}, bf16[6...) custom-call(f32[33]{0:T(128)} %grid_x.1, f32[33]{0:T(128)} %test_x.1, f32[33,256]{1,0:T(8,128)} %bitcast.17, ...), custom_call_target="tpu_custom_call" | custom-call | flops 2000000000 | bytes 1000000 | tf_op jit(solution)/shard_map/pallas_call | solution.py:220
  19.7 0.0 copy-start
  19.7 0.0 copy-start.2
  19.7 0.0 copy-start.4
  19.7 0.0 copy-start.5
  19.7 0.0 collective-permute-done.1.x_second
  19.7 0.0 collective-permute-done.x_first
  19.7 0.0 copy-done.7
  19.7 0.0 copy-done.8
  19.7 0.3 shard_map.68
  20.1 5.5 %collective-permute-start.2 = (f32[296,128]{1,0:T(8,128)S(1)}, f32[296,128]{1,0:T(8,128)S(1)}, u32[]{:S(2)}, u32[]{:S(2)}) collective-permute-start(f32[296,128]{1,0:T(8,128)S(1)} %get-tuple-element.23), channel_id=1, source_target_pairs={{1,2},{3,4},{5,6},{7,8},{9,10},{11,12},{13,14},{2,1},{4,3},{6,5},{... | collective-permute-start | bytes 454664 | tf_op jit(solution)/shard_map/ppermute | solution.py:412
  25.6 1.9 %collective-permute-start.3 = (f32[296,128]{1,0:T(8,128)S(1)}, f32[296,128]{1,0:T(8,128)S(1)}, u32[]{:S(2)}, u32[]{:S(2)}) collective-permute-start(f32[296,128]{1,0:T(8,128)S(1)} %get-tuple-element.24), channel_id=1, source_target_pairs={{0,1},{2,3},{4,5},{6,7},{8,9},{10,11},{12,13},{14,15},{1,0},{3,2},... | collective-permute-start | bytes 454664 | tf_op jit(solution)/shard_map/ppermute | solution.py:413
  27.5 0.0 copy-done
  27.5 0.0 copy-done.2
  27.5 0.0 copy-done.4
  27.5 0.0 copy-done.5
  27.5 0.0 copy-start.1
  27.5 0.0 copy-start.3
  27.5 0.0 copy-start.6
  27.6 2.6 %shard_map.70 = (f32[2976,256]{1,0:T(8,128)S(1)}, bf16[3,352,128]{2,1,0:T(8,128)(2,1)S(1)}) custom-call(f32[3,384,256]{2,1,0:T(8,128)S(1)} %get-tuple-element.16.read, bf16[128,512]{1,0:T(8,128)(2,1)S(1)} %copy-done.2, bf16[96,384]{1,0:T(8,128)(2,1)S(1)} %copy-done.4, bf16[64,384]{1,0:T(8,128)(2,1)S(1)} %copy-done.5, bf16[1024,256]{1,0:T(8,128)(2,1)S(1)} %copy-done), custom_call_target="tpu_custom_call" | custom-call | flops 3000000000 | bytes 1000000 | tf_op jit(solution)/shard_map/pallas_call | solution.py:270
  30.2 0.0 collective-permute-done.2.y_first
  30.2 0.0 collective-permute-done.3.y_second
  30.2 0.0 copy-done.1
  30.2 0.0 copy-done.3
  30.2 0.0 copy-done.6
  30.3 5.6 %shard_map.71 = (f32[6,320,256]{2,1,0:T(8,128)}, f32[6,320,256]{2,1,0:T(8,128)}) custom-call(f32[2976,256]{1,0:T(8,128)S(1)} %get-tuple-element.21.part, bf16[3,352,128]{2,1,0:T(8,128)(2,1)S(1)} %get-tuple-element.22.ends, f32[296,128]{1,0:T(8,128)S(1)} %collective-permute-done.2.y_first, f32[296,128]{1,0:T(8,128)S(1)} %collective-permute-done.3.y_second, ...), custom_call_target="tpu_custom_call" | custom-call | tf_op jit(solution)/shard_map/pallas_call | solution.py:376
Async XLA Ops:
  1.6 18.1 %collective-permute-start.1 = (f32[3,32,256]{2,1,0:T(8,128)S(1)}, f32[3,32,256]{2,1,0:T(8,128)S(1)}, u32[]{:S(2)}, u32[]{:S(2)}) collective-permute-start(f32[3,32,256]{2,1,0:T(8,128)S(1)} %get-tuple-element.32), channel_id=1, source_target_pairs={{0,16},{32,48},{64,80},{96,112},{128,144},{160,176},{192,208},{224... | collective-permute-start | bytes 294920 | tf_op jit(solution)/shard_map/ppermute | solution.py:409
  6.0 13.7 %collective-permute-start = (f32[3,32,256]{2,1,0:T(8,128)S(1)}, f32[3,32,256]{2,1,0:T(8,128)S(1)}, u32[]{:S(2)}, u32[]{:S(2)}) collective-permute-start(f32[3,32,256]{2,1,0:T(8,128)S(1)} %get-tuple-element.33), channel_id=1, source_target_pairs={{16,32},{48,64},{80,96},{112,128},{144,160},{176,192},{208,224},{2... | collective-permute-start | bytes 294920 | tf_op jit(solution)/shard_map/ppermute | solution.py:408
  17.1 2.6 %copy-start.7 = (f32[3,1,256,320]{2,3,1,0:T(8,128)S(1)}, f32[3,1,256,320]{2,3,1,0:T(8,128)}, u32[]{:S(2)}) copy-start(f32[3,1,256,320]{2,3,1,0:T(8,128)} %param.5) | copy-start | bytes 2949124
  17.1 2.6 %copy-start.8 = (f32[256,33]{0,1:T(8,128)S(1)}, f32[256,33]{0,1:T(8,128)}, u32[]{:S(2)}) copy-start(f32[256,33]{0,1:T(8,128)} %param.7) | copy-start | bytes 101380
  19.7 7.8 %copy-start = (bf16[1024,256]{1,0:T(8,128)(2,1)S(1)}, bf16[1024,256]{1,0:T(8,128)(2,1)}, u32[]{:S(2)}) copy-start(bf16[1024,256]{1,0:T(8,128)(2,1)} %get-tuple-element.20.y_grid) | copy-start | bytes 1572868
  19.7 7.8 %copy-start.2 = (bf16[128,512]{1,0:T(8,128)(2,1)S(1)}, bf16[128,512]{1,0:T(8,128)(2,1)}, u32[]{:S(2)}) copy-start(bf16[128,512]{1,0:T(8,128)(2,1)} %get-tuple-element.17.x128) | copy-start | bytes 393220
  19.7 7.8 %copy-start.4 = (bf16[96,384]{1,0:T(8,128)(2,1)S(1)}, bf16[96,384]{1,0:T(8,128)(2,1)}, u32[]{:S(2)}) copy-start(bf16[96,384]{1,0:T(8,128)(2,1)} %get-tuple-element.18.x96) | copy-start | bytes 221188
  19.7 7.8 %copy-start.5 = (bf16[64,384]{1,0:T(8,128)(2,1)S(1)}, bf16[64,384]{1,0:T(8,128)(2,1)}, u32[]{:S(2)}) copy-start(bf16[64,384]{1,0:T(8,128)(2,1)} %get-tuple-element.19.x64) | copy-start | bytes 147460
  20.1 10.1 %collective-permute-start.2 = (f32[296,128]{1,0:T(8,128)S(1)}, f32[296,128]{1,0:T(8,128)S(1)}, u32[]{:S(2)}, u32[]{:S(2)}) collective-permute-start(f32[296,128]{1,0:T(8,128)S(1)} %get-tuple-element.23), channel_id=1, source_target_pairs={{1,2},{3,4},{5,6},{7,8},{9,10},{11,12},{13,14},{2,1},{4,3},{6,5},{... | collective-permute-start | bytes 454664 | tf_op jit(solution)/shard_map/ppermute | solution.py:412
  25.6 4.7 %collective-permute-start.3 = (f32[296,128]{1,0:T(8,128)S(1)}, f32[296,128]{1,0:T(8,128)S(1)}, u32[]{:S(2)}, u32[]{:S(2)}) collective-permute-start(f32[296,128]{1,0:T(8,128)S(1)} %get-tuple-element.24), channel_id=1, source_target_pairs={{0,1},{2,3},{4,5},{6,7},{8,9},{10,11},{12,13},{14,15},{1,0},{3,2},... | collective-permute-start | bytes 454664 | tf_op jit(solution)/shard_map/ppermute | solution.py:413
  27.5 2.7 %copy-start.1 = (bf16[1024,256]{1,0:T(8,128)(2,1)S(1)}, bf16[1024,256]{1,0:T(8,128)(2,1)}, u32[]{:S(2)}) copy-start(bf16[1024,256]{1,0:T(8,128)(2,1)} %get-tuple-element.25.y_test) | copy-start | bytes 1572868
  27.5 2.7 %copy-start.3 = (bf16[128,512]{1,0:T(8,128)(2,1)S(1)}, bf16[128,512]{1,0:T(8,128)(2,1)}, u32[]{:S(2)}) copy-start(bf16[128,512]{1,0:T(8,128)(2,1)} %get-tuple-element.26.t128) | copy-start | bytes 393220
  27.5 2.7 %copy-start.6 = (bf16[64,384]{1,0:T(8,128)(2,1)S(1)}, bf16[64,384]{1,0:T(8,128)(2,1)}, u32[]{:S(2)}) copy-start(bf16[64,384]{1,0:T(8,128)(2,1)} %get-tuple-element.27.t64) | copy-start | bytes 147460
